TPU v7x, 32 devices: a whole 2x2x4 slice. The times are simulated.
32 devices in a mesh: fsdp: 32 (over z, y, x, core).
Axes of the slice: x: 2, y: 2, z: 4, core: 2. Of those that a mesh axis runs over, the one named last changes fastest.
Arguments:
- patches: bfloat16 [12288, 768], P('fsdp'), may hold values from -6 to 6
- visible_index: int32 [12288], P('fsdp'), may hold values from 0 to 528, as said below
- segments: int32 [16928], P('fsdp'), may hold values from 0 to 1, as said below
- cotangent: bfloat16 [16928, 512], P('fsdp'), may hold values from -6 to 6
- enc_norm1_gain: bfloat16 [768], P('fsdp'), may hold values from 0.25 to 1.75
- enc_norm1_bias: bfloat16 [768], P('fsdp'), may hold values from -1.5 to 1.5
- enc_qkv: bfloat16 [768, 2304], P('fsdp'), may hold values from -0.21875 to 0.21875
- enc_query_bias: bfloat16 [768], P('fsdp'), may hold values from -1.5 to 1.5
- enc_value_bias: bfloat16 [768], P('fsdp'), may hold values from -1.5 to 1.5
- enc_out: bfloat16 [768, 768], P('fsdp'), may hold values from -0.875 to 0.875
- enc_out_bias: bfloat16 [768], P('fsdp'), may hold values from -1.5 to 1.5
- enc_norm2_gain: bfloat16 [768], P('fsdp'), may hold values from 0.25 to 1.75
- enc_norm2_bias: bfloat16 [768], P('fsdp'), may hold values from -1.5 to 1.5
- enc_up: bfloat16 [768, 3072], P('fsdp'), may hold values from -0.21875 to 0.21875
- enc_up_bias: bfloat16 [3072], P('fsdp'), may hold values from -2.5 to 2.5
- enc_down: bfloat16 [3072, 768], P('fsdp'), may hold values from -0.109375 to 0.109375
- enc_down_bias: bfloat16 [768], P('fsdp'), may hold values from -1.5 to 1.5
- embed_weight: bfloat16 [768, 512], P('fsdp'), may hold values from -0.21875 to 0.21875
- embed_bias: bfloat16 [512], P('fsdp'), may hold values from -1.5 to 1.5
- mask_token: bfloat16 [512], P('fsdp'), may hold values from -4 to 4
- dec_norm1_gain: bfloat16 [512], P('fsdp'), may hold values from 0.25 to 1.75
- dec_norm1_bias: bfloat16 [512], P('fsdp'), may hold values from -1.5 to 1.5
- dec_qkv: bfloat16 [512, 1536], P('fsdp'), may hold values from -0.25 to 0.25
- dec_query_bias: bfloat16 [512], P('fsdp'), may hold values from -1.5 to 1.5
- dec_value_bias: bfloat16 [512], P('fsdp'), may hold values from -1.5 to 1.5
- dec_out: bfloat16 [512, 512], P('fsdp'), may hold values from -1 to 1
- dec_out_bias: bfloat16 [512], P('fsdp'), may hold values from -1.5 to 1.5
- dec_norm2_gain: bfloat16 [512], P('fsdp'), may hold values from 0.25 to 1.75
- dec_norm2_bias: bfloat16 [512], P('fsdp'), may hold values from -1.5 to 1.5
- dec_up: bfloat16 [512, 2048], P('fsdp'), may hold values from -0.25 to 0.25
- dec_up_bias: bfloat16 [2048], P('fsdp'), may hold values from -2.5 to 2.5
- dec_down: bfloat16 [2048, 512], P('fsdp'), may hold values from -0.125 to 0.125
- dec_down_bias: bfloat16 [512], P('fsdp'), may hold values from -1.5 to 1.5
Outputs:
- decoder_out: bfloat16 [16928, 512], P('fsdp')
- patch_grad: float32 [12288, 768], P('fsdp')
- grad_enc_norm1_gain: float32 [768], P('fsdp')
- grad_enc_norm1_bias: float32 [768], P('fsdp')
- grad_enc_qkv: float32 [768, 2304], P('fsdp')
- grad_enc_query_bias: float32 [768], P('fsdp')
- grad_enc_value_bias: float32 [768], P('fsdp')
- grad_enc_out: float32 [768, 768], P('fsdp')
- grad_enc_out_bias: float32 [768], P('fsdp')
- grad_enc_norm2_gain: float32 [768], P('fsdp')
- grad_enc_norm2_bias: float32 [768], P('fsdp')
- grad_enc_up: float32 [768, 3072], P('fsdp')
- grad_enc_up_bias: float32 [3072], P('fsdp')
- grad_enc_down: float32 [3072, 768], P('fsdp')
- grad_enc_down_bias: float32 [768], P('fsdp')
- grad_embed_weight: float32 [768, 512], P('fsdp')
- grad_embed_bias: float32 [512], P('fsdp')
- grad_mask_token: float32 [512], P('fsdp')
- grad_dec_norm1_gain: float32 [512], P('fsdp')
- grad_dec_norm1_bias: float32 [512], P('fsdp')
- grad_dec_qkv: float32 [512, 1536], P('fsdp')
- grad_dec_query_bias: float32 [512], P('fsdp')
- grad_dec_value_bias: float32 [512], P('fsdp')
- grad_dec_out: float32 [512, 512], P('fsdp')
- grad_dec_out_bias: float32 [512], P('fsdp')
- grad_dec_norm2_gain: float32 [512], P('fsdp')
- grad_dec_norm2_bias: float32 [512], P('fsdp')
- grad_dec_up: float32 [512, 2048], P('fsdp')
- grad_dec_up_bias: float32 [2048], P('fsdp')
- grad_dec_down: float32 [2048, 512], P('fsdp')
- grad_dec_down_bias: float32 [512], P('fsdp')
Inputs may be any that keep to these rules, and one draw needn't show every extreme that they name: `visible_index`: each sequence's block of 384 entries names distinct slots of that sequence in ascending order; its other 145 slots are masked. `segments`: each sequence of 529 slots is either one document (all ids 0) or two packed ones: id 0 on its first 264 slots and 1 on the rest.
All inputs are finite; a program needn't handle non-finite values.
Results may differ from a plain program's by a relative error of at most 0.025.
Values may be sent and summed in bfloat16 or wider, within the bound.
A program may use at most 256 MiB of HBM per device.

v0:
```python
import jax
import jax.numpy as jnp
from jax import lax
from jax.sharding import PartitionSpec as P

HEADS = 12
DD = 512
DHEADS = 16
ROW = 529
VIS = 384


EPSILON = 1e-06


def widen(value):
    return value.astype(jnp.float32)


def layer_norm(stream, gain, shift):
    row_mean = jnp.mean(stream, -1, keepdims=True)
    centred = stream - row_mean
    row_var = jnp.mean(centred * centred, -1, keepdims=True)
    return centred * lax.rsqrt(row_var + EPSILON) * gain + shift


def norm_back(stream, gain, shift, grad_out):
    pull = jax.vjp(layer_norm, stream, gain, shift)[1]
    return pull(grad_out)


def gelu_exact(value):
    return jax.nn.gelu(value, approximate=False)


def split_heads(rows, head_count):
    batch, length, model_width = rows.shape
    return rows.reshape(batch, length, head_count, model_width // head_count)


def masked_scores(query_heads, key_heads, same_doc, score_scale):
    scores = (
        jnp.einsum("bqhd,bkhd->bhqk", query_heads, key_heads, preferred_element_type=jnp.float32)
        * score_scale
    )
    return jnp.where(same_doc[:, None], scores, -1000000000.0)


def attend_forward(query_rows, key_rows, value_rows, same_doc, head_count, score_scale):
    batch, length, model_width = query_rows.shape
    scores = masked_scores(
        split_heads(query_rows, head_count),
        split_heads(key_rows, head_count),
        same_doc,
        score_scale,
    )
    row_max = jnp.max(scores, -1, keepdims=True)
    expo = jnp.exp(scores - row_max)
    row_sum = jnp.sum(expo, -1, keepdims=True)
    att_probs = (expo / row_sum).astype(jnp.bfloat16)
    mixed = jnp.einsum(
        "bhqk,bkhd->bqhd",
        att_probs,
        split_heads(value_rows, head_count),
        preferred_element_type=jnp.float32,
    )
    return (mixed.reshape(batch, length, model_width), row_max + jnp.log(row_sum))


def attend_backward(
    query_rows, key_rows, value_rows, same_doc, log_total, grad_mixed, head_count, score_scale
):
    batch, length, model_width = query_rows.shape
    query_heads = split_heads(query_rows, head_count)
    key_heads = split_heads(key_rows, head_count)
    value_heads = split_heads(value_rows, head_count)
    grad_heads = split_heads(grad_mixed, head_count)
    att_probs = jnp.exp(masked_scores(query_heads, key_heads, same_doc, score_scale) - log_total)
    grad_value = jnp.einsum(
        "bhqk,bqhd->bkhd",
        att_probs.astype(jnp.bfloat16),
        grad_heads,
        preferred_element_type=jnp.float32,
    )
    grad_probs = jnp.einsum(
        "bqhd,bkhd->bhqk", grad_heads, value_heads, preferred_element_type=jnp.float32
    )
    centre = jnp.sum(att_probs * grad_probs, -1, keepdims=True)
    grad_scores = (att_probs * (grad_probs - centre) * score_scale).astype(jnp.bfloat16)
    grad_query = jnp.einsum(
        "bhqk,bkhd->bqhd", grad_scores, key_heads, preferred_element_type=jnp.float32
    )
    grad_key = jnp.einsum(
        "bhqk,bqhd->bkhd", grad_scores, query_heads, preferred_element_type=jnp.float32
    )
    rows = batch * length
    return (
        grad_query.reshape(rows, model_width),
        grad_key.reshape(rows, model_width),
        grad_value.reshape(rows, model_width),
    )


def block_forward(stream, params, seg_ids, head_count):
    (
        gain_one,
        shift_one,
        w_qkv,
        query_bias,
        value_bias,
        w_out,
        out_bias,
        gain_two,
        shift_two,
        w_up,
        up_bias,
        w_down,
        down_bias,
    ) = params
    row_count, model_width = stream.shape
    batch, length = seg_ids.shape
    score_scale = (model_width // head_count) ** (-0.5)
    normed = layer_norm(stream, widen(gain_one), widen(shift_one)).astype(jnp.bfloat16)
    joined = jnp.dot(normed, w_qkv, preferred_element_type=jnp.float32)
    query_rows = (joined[:, :model_width] + widen(query_bias)).astype(jnp.bfloat16)
    key_rows = joined[:, model_width : 2 * model_width].astype(jnp.bfloat16)
    value_rows = (joined[:, 2 * model_width :] + widen(value_bias)).astype(jnp.bfloat16)
    same_doc = seg_ids[:, :, None] == seg_ids[:, None, :]
    shape_three = (batch, length, model_width)
    mixed, log_total = attend_forward(
        query_rows.reshape(shape_three),
        key_rows.reshape(shape_three),
        value_rows.reshape(shape_three),
        same_doc,
        head_count,
        score_scale,
    )
    attended = mixed.reshape(row_count, model_width).astype(jnp.bfloat16)
    middle = stream + jnp.dot(attended, w_out, preferred_element_type=jnp.float32) + widen(out_bias)
    normed_two = layer_norm(middle, widen(gain_two), widen(shift_two)).astype(jnp.bfloat16)
    hidden_up = jnp.dot(normed_two, w_up, preferred_element_type=jnp.float32) + widen(up_bias)
    activated = gelu_exact(hidden_up).astype(jnp.bfloat16)
    result = (
        middle + jnp.dot(activated, w_down, preferred_element_type=jnp.float32) + widen(down_bias)
    )
    saved = (
        stream,
        middle,
        normed,
        query_rows,
        key_rows,
        value_rows,
        log_total,
        attended,
        normed_two,
        hidden_up,
        activated,
    )
    return (result, saved)


def back_feed(grad_out, params, saved):
    (
        gain_one,
        shift_one,
        w_qkv,
        query_bias,
        value_bias,
        w_out,
        out_bias,
        gain_two,
        shift_two,
        w_up,
        up_bias,
        w_down,
        down_bias,
    ) = params
    (
        stream,
        middle,
        normed,
        query_rows,
        key_rows,
        value_rows,
        log_total,
        attended,
        normed_two,
        hidden_up,
        activated,
    ) = saved
    grad_low = grad_out.astype(jnp.bfloat16)
    grad_down_bias = jnp.sum(grad_out, 0)
    grad_down = jnp.einsum("rf,rw->fw", activated, grad_low, preferred_element_type=jnp.float32)
    grad_act = jnp.einsum("rw,fw->rf", grad_low, w_down, preferred_element_type=jnp.float32)
    grad_hidden = jax.vjp(gelu_exact, hidden_up)[1](grad_act)[0]
    grad_hidden_low = grad_hidden.astype(jnp.bfloat16)
    grad_up_bias = jnp.sum(grad_hidden, 0)
    grad_up = jnp.einsum(
        "rd,rf->df", normed_two, grad_hidden_low, preferred_element_type=jnp.float32
    )
    grad_normed_two = jnp.einsum(
        "rf,df->rd", grad_hidden_low, w_up, preferred_element_type=jnp.float32
    )
    grad_mid_norm, grad_gain_two, grad_shift_two = norm_back(
        middle, widen(gain_two), widen(shift_two), grad_normed_two
    )
    grad_middle = grad_out + grad_mid_norm
    return (
        grad_middle,
        (grad_gain_two, grad_shift_two, grad_up, grad_up_bias, grad_down, grad_down_bias),
    )


def back_attend(grad_middle, params, seg_ids, head_count, saved):
    (
        gain_one,
        shift_one,
        w_qkv,
        query_bias,
        value_bias,
        w_out,
        out_bias,
        gain_two,
        shift_two,
        w_up,
        up_bias,
        w_down,
        down_bias,
    ) = params
    (
        stream,
        middle,
        normed,
        query_rows,
        key_rows,
        value_rows,
        log_total,
        attended,
        normed_two,
        hidden_up,
        activated,
    ) = saved
    row_count, model_width = stream.shape
    batch, length = seg_ids.shape
    score_scale = (model_width // head_count) ** (-0.5)
    grad_middle_low = grad_middle.astype(jnp.bfloat16)
    grad_out_bias = jnp.sum(grad_middle, 0)
    grad_w_out = jnp.einsum(
        "rv,rw->vw", attended, grad_middle_low, preferred_element_type=jnp.float32
    )
    grad_attended = jnp.einsum(
        "rw,vw->rv", grad_middle_low, w_out, preferred_element_type=jnp.float32
    ).astype(jnp.bfloat16)
    same_doc = seg_ids[:, :, None] == seg_ids[:, None, :]
    shape_three = (batch, length, model_width)
    grad_query, grad_key, grad_value = attend_backward(
        query_rows.reshape(shape_three),
        key_rows.reshape(shape_three),
        value_rows.reshape(shape_three),
        same_doc,
        log_total,
        grad_attended.reshape(shape_three),
        head_count,
        score_scale,
    )
    grad_query_bias = jnp.sum(grad_query, 0)
    grad_value_bias = jnp.sum(grad_value, 0)
    grad_joined = jnp.concatenate([grad_query, grad_key, grad_value], 1).astype(jnp.bfloat16)
    grad_qkv = jnp.einsum("rd,rc->dc", normed, grad_joined, preferred_element_type=jnp.float32)
    grad_normed = jnp.einsum("rc,dc->rd", grad_joined, w_qkv, preferred_element_type=jnp.float32)
    grad_in_norm, grad_gain_one, grad_shift_one = norm_back(
        stream, widen(gain_one), widen(shift_one), grad_normed
    )
    grads = (
        grad_gain_one,
        grad_shift_one,
        grad_qkv,
        grad_query_bias,
        grad_value_bias,
        grad_w_out,
        grad_out_bias,
    )
    return (grad_middle + grad_in_norm, grads)


def block_backward(grad_out, params, seg_ids, head_count, saved):
    grad_middle, feed_grads = back_feed(grad_out, params, saved)
    grad_in, attend_grads = back_attend(grad_middle, params, seg_ids, head_count, saved)
    return (grad_in, attend_grads + feed_grads)


def on_device(
    patches,
    visible_index,
    segments,
    cotangent,
    enc_norm1_gain,
    enc_norm1_bias,
    enc_qkv,
    enc_query_bias,
    enc_value_bias,
    enc_out,
    enc_out_bias,
    enc_norm2_gain,
    enc_norm2_bias,
    enc_up,
    enc_up_bias,
    enc_down,
    enc_down_bias,
    embed_weight,
    embed_bias,
    mask_token,
    dec_norm1_gain,
    dec_norm1_bias,
    dec_qkv,
    dec_query_bias,
    dec_value_bias,
    dec_out,
    dec_out_bias,
    dec_norm2_gain,
    dec_norm2_bias,
    dec_up,
    dec_up_bias,
    dec_down,
    dec_down_bias,
):
    seq_count = segments.shape[0] // ROW
    seg_ids = segments.reshape(seq_count, ROW)
    vis_slots = visible_index.reshape(seq_count, VIS)
    enc_seg = jnp.take_along_axis(seg_ids, vis_slots, 1)
    seq_index = jnp.arange(seq_count, dtype=jnp.int32)[:, None]
    enc_full = (
        lax.all_gather(enc_norm1_gain, "fsdp", axis=0, tiled=True),
        lax.all_gather(enc_norm1_bias, "fsdp", axis=0, tiled=True),
        lax.all_gather(enc_qkv, "fsdp", axis=0, tiled=True),
        lax.all_gather(enc_query_bias, "fsdp", axis=0, tiled=True),
        lax.all_gather(enc_value_bias, "fsdp", axis=0, tiled=True),
        lax.all_gather(enc_out, "fsdp", axis=0, tiled=True),
        lax.all_gather(enc_out_bias, "fsdp", axis=0, tiled=True),
        lax.all_gather(enc_norm2_gain, "fsdp", axis=0, tiled=True),
        lax.all_gather(enc_norm2_bias, "fsdp", axis=0, tiled=True),
        lax.all_gather(enc_up, "fsdp", axis=0, tiled=True),
        lax.all_gather(enc_up_bias, "fsdp", axis=0, tiled=True),
        lax.all_gather(enc_down, "fsdp", axis=0, tiled=True),
        lax.all_gather(enc_down_bias, "fsdp", axis=0, tiled=True),
    )
    hidden, enc_saved = block_forward(widen(patches), enc_full, enc_seg, HEADS)
    dec_full = (
        lax.all_gather(embed_weight, "fsdp", axis=0, tiled=True),
        lax.all_gather(embed_bias, "fsdp", axis=0, tiled=True),
        lax.all_gather(mask_token, "fsdp", axis=0, tiled=True),
        lax.all_gather(dec_norm1_gain, "fsdp", axis=0, tiled=True),
        lax.all_gather(dec_norm1_bias, "fsdp", axis=0, tiled=True),
        lax.all_gather(dec_qkv, "fsdp", axis=0, tiled=True),
        lax.all_gather(dec_query_bias, "fsdp", axis=0, tiled=True),
        lax.all_gather(dec_value_bias, "fsdp", axis=0, tiled=True),
        lax.all_gather(dec_out, "fsdp", axis=0, tiled=True),
        lax.all_gather(dec_out_bias, "fsdp", axis=0, tiled=True),
        lax.all_gather(dec_norm2_gain, "fsdp", axis=0, tiled=True),
        lax.all_gather(dec_norm2_bias, "fsdp", axis=0, tiled=True),
        lax.all_gather(dec_up, "fsdp", axis=0, tiled=True),
        lax.all_gather(dec_up_bias, "fsdp", axis=0, tiled=True),
        lax.all_gather(dec_down, "fsdp", axis=0, tiled=True),
        lax.all_gather(dec_down_bias, "fsdp", axis=0, tiled=True),
    )
    hidden_low = hidden.astype(jnp.bfloat16)
    embedded = jnp.dot(hidden_low, dec_full[0], preferred_element_type=jnp.float32) + widen(
        dec_full[1]
    )
    embedded = embedded.reshape(seq_count, VIS, DD)
    dec_in = (
        jnp.broadcast_to(widen(dec_full[2]), (seq_count, ROW, DD))
        .at[seq_index, vis_slots]
        .set(embedded)
    )
    dec_in = dec_in.reshape(seq_count * ROW, DD)
    decoded, dec_saved = block_forward(dec_in, dec_full[3:], seg_ids, DHEADS)
    dec_back = (
        lax.all_gather(embed_weight, "fsdp", axis=0, tiled=True),
        lax.all_gather(embed_bias, "fsdp", axis=0, tiled=True),
        lax.all_gather(mask_token, "fsdp", axis=0, tiled=True),
        lax.all_gather(dec_norm1_gain, "fsdp", axis=0, tiled=True),
        lax.all_gather(dec_norm1_bias, "fsdp", axis=0, tiled=True),
        lax.all_gather(dec_qkv, "fsdp", axis=0, tiled=True),
        lax.all_gather(dec_query_bias, "fsdp", axis=0, tiled=True),
        lax.all_gather(dec_value_bias, "fsdp", axis=0, tiled=True),
        lax.all_gather(dec_out, "fsdp", axis=0, tiled=True),
        lax.all_gather(dec_out_bias, "fsdp", axis=0, tiled=True),
        lax.all_gather(dec_norm2_gain, "fsdp", axis=0, tiled=True),
        lax.all_gather(dec_norm2_bias, "fsdp", axis=0, tiled=True),
        lax.all_gather(dec_up, "fsdp", axis=0, tiled=True),
        lax.all_gather(dec_up_bias, "fsdp", axis=0, tiled=True),
        lax.all_gather(dec_down, "fsdp", axis=0, tiled=True),
        lax.all_gather(dec_down_bias, "fsdp", axis=0, tiled=True),
    )
    grad_dec_in, dec_grads = block_backward(
        widen(cotangent), dec_back[3:], seg_ids, DHEADS, dec_saved
    )
    grad_dec_in = grad_dec_in.reshape(seq_count, ROW, DD)
    shown_slots = jnp.zeros((seq_count, ROW), jnp.float32).at[seq_index, vis_slots].set(1.0)
    grad_mask = jnp.sum((1.0 - shown_slots)[:, :, None] * grad_dec_in, (0, 1))
    grad_embedded = grad_dec_in[seq_index, vis_slots].reshape(seq_count * VIS, DD)
    grad_embed_b = jnp.sum(grad_embedded, 0)
    grad_embedded_low = grad_embedded.astype(jnp.bfloat16)
    grad_embed_w = jnp.einsum(
        "rd,re->de", hidden_low, grad_embedded_low, preferred_element_type=jnp.float32
    )
    grad_hidden = jnp.einsum(
        "re,de->rd", grad_embedded_low, dec_back[0], preferred_element_type=jnp.float32
    )
    dec_sums = (
        lax.psum_scatter(grad_embed_w, "fsdp", scatter_dimension=0, tiled=True),
        lax.psum_scatter(grad_embed_b, "fsdp", scatter_dimension=0, tiled=True),
        lax.psum_scatter(grad_mask, "fsdp", scatter_dimension=0, tiled=True),
        lax.psum_scatter(dec_grads[0], "fsdp", scatter_dimension=0, tiled=True),
        lax.psum_scatter(dec_grads[1], "fsdp", scatter_dimension=0, tiled=True),
        lax.psum_scatter(dec_grads[2], "fsdp", scatter_dimension=0, tiled=True),
        lax.psum_scatter(dec_grads[3], "fsdp", scatter_dimension=0, tiled=True),
        lax.psum_scatter(dec_grads[4], "fsdp", scatter_dimension=0, tiled=True),
        lax.psum_scatter(dec_grads[5], "fsdp", scatter_dimension=0, tiled=True),
        lax.psum_scatter(dec_grads[6], "fsdp", scatter_dimension=0, tiled=True),
        lax.psum_scatter(dec_grads[7], "fsdp", scatter_dimension=0, tiled=True),
        lax.psum_scatter(dec_grads[8], "fsdp", scatter_dimension=0, tiled=True),
        lax.psum_scatter(dec_grads[9], "fsdp", scatter_dimension=0, tiled=True),
        lax.psum_scatter(dec_grads[10], "fsdp", scatter_dimension=0, tiled=True),
        lax.psum_scatter(dec_grads[11], "fsdp", scatter_dimension=0, tiled=True),
        lax.psum_scatter(dec_grads[12], "fsdp", scatter_dimension=0, tiled=True),
    )
    enc_back = (
        lax.all_gather(enc_norm1_gain, "fsdp", axis=0, tiled=True),
        lax.all_gather(enc_norm1_bias, "fsdp", axis=0, tiled=True),
        lax.all_gather(enc_qkv, "fsdp", axis=0, tiled=True),
        lax.all_gather(enc_query_bias, "fsdp", axis=0, tiled=True),
        lax.all_gather(enc_value_bias, "fsdp", axis=0, tiled=True),
        lax.all_gather(enc_out, "fsdp", axis=0, tiled=True),
        lax.all_gather(enc_out_bias, "fsdp", axis=0, tiled=True),
        lax.all_gather(enc_norm2_gain, "fsdp", axis=0, tiled=True),
        lax.all_gather(enc_norm2_bias, "fsdp", axis=0, tiled=True),
        lax.all_gather(enc_up, "fsdp", axis=0, tiled=True),
        lax.all_gather(enc_up_bias, "fsdp", axis=0, tiled=True),
        lax.all_gather(enc_down, "fsdp", axis=0, tiled=True),
        lax.all_gather(enc_down_bias, "fsdp", axis=0, tiled=True),
    )
    grad_patches, enc_grads = block_backward(grad_hidden, enc_back, enc_seg, HEADS, enc_saved)
    enc_sums = (
        lax.psum_scatter(enc_grads[0], "fsdp", scatter_dimension=0, tiled=True),
        lax.psum_scatter(enc_grads[1], "fsdp", scatter_dimension=0, tiled=True),
        lax.psum_scatter(enc_grads[2], "fsdp", scatter_dimension=0, tiled=True),
        lax.psum_scatter(enc_grads[3], "fsdp", scatter_dimension=0, tiled=True),
        lax.psum_scatter(enc_grads[4], "fsdp", scatter_dimension=0, tiled=True),
        lax.psum_scatter(enc_grads[5], "fsdp", scatter_dimension=0, tiled=True),
        lax.psum_scatter(enc_grads[6], "fsdp", scatter_dimension=0, tiled=True),
        lax.psum_scatter(enc_grads[7], "fsdp", scatter_dimension=0, tiled=True),
        lax.psum_scatter(enc_grads[8], "fsdp", scatter_dimension=0, tiled=True),
        lax.psum_scatter(enc_grads[9], "fsdp", scatter_dimension=0, tiled=True),
        lax.psum_scatter(enc_grads[10], "fsdp", scatter_dimension=0, tiled=True),
        lax.psum_scatter(enc_grads[11], "fsdp", scatter_dimension=0, tiled=True),
        lax.psum_scatter(enc_grads[12], "fsdp", scatter_dimension=0, tiled=True),
    )
    return (decoded.astype(jnp.bfloat16), grad_patches) + tuple(enc_sums) + tuple(dec_sums)


def solution(mesh):
    return jax.shard_map(
        on_device,
        mesh=mesh,
        in_specs=(
            P("fsdp", None),
            P("fsdp"),
            P("fsdp"),
            P("fsdp", None),
            P("fsdp"),
            P("fsdp"),
            P("fsdp", None),
            P("fsdp"),
            P("fsdp"),
            P("fsdp", None),
            P("fsdp"),
            P("fsdp"),
            P("fsdp"),
            P("fsdp", None),
            P("fsdp"),
            P("fsdp", None),
            P("fsdp"),
            P("fsdp", None),
            P("fsdp"),
            P("fsdp"),
            P("fsdp"),
            P("fsdp"),
            P("fsdp", None),
            P("fsdp"),
            P("fsdp"),
            P("fsdp", None),
            P("fsdp"),
            P("fsdp"),
            P("fsdp"),
            P("fsdp", None),
            P("fsdp"),
            P("fsdp", None),
            P("fsdp"),
        ),
        out_specs=(
            P("fsdp", None),
            P("fsdp", None),
            P("fsdp"),
            P("fsdp"),
            P("fsdp", None),
            P("fsdp"),
            P("fsdp"),
            P("fsdp", None),
            P("fsdp"),
            P("fsdp"),
            P("fsdp"),
            P("fsdp", None),
            P("fsdp"),
            P("fsdp", None),
            P("fsdp"),
            P("fsdp", None),
            P("fsdp"),
            P("fsdp"),
            P("fsdp"),
            P("fsdp"),
            P("fsdp", None),
            P("fsdp"),
            P("fsdp"),
            P("fsdp", None),
            P("fsdp"),
            P("fsdp"),
            P("fsdp"),
            P("fsdp", None),
            P("fsdp"),
            P("fsdp", None),
            P("fsdp"),
        ),
        check_vma=False,
    )
```

profile of v0, /device:TPU:0, one launch (start us, length us, event | category | flops | bytes accessed | tf_op | source)
XLA Modules:
  0.0 1922.0 jit_solution(17658119743186661566)
XLA Ops:
  28.6 43.4 %all-reduce.42 = (bf16[512]{0:T(512)(128)(2,1)}, bf16[768]{0:T(1024)(128)(2,1)S(1)}, bf16[768]{0:T(1024)(128)(2,1)S(1)}, bf16[768]{0:T(1024)(128)(2,1)S(1)}, bf1...) all-reduce(bf16[512]{0:T(512)(128)(2,1)S(1)} %dynamic-update-slice,, ...), channel_id=1, replica_groups=mesh['fsdp'=32] {'fsdp'}, use_global_device_ids=true, to_apply=%add.1 | all-reduce | flops 16384 | bytes 65536
  74.8 42.2 %all_gather.121 = bf16[512,512]{1,0:T(8,128)(2,1)S(1)} all-gather(bf16[16,512]{1,0:T(8,128)(2,1)S(1)} %copy-done.71), channel_id=1, replica_groups=mesh['fsdp'=32] {'fsdp'}, dimensions={0}, use_global_device_ids=true | all-gather | bytes 540672 | tf_op jit(solution)/shard_map/all_gather | solution.py:357
  117.0 39.3 %all_gather.114 = bf16[768,512]{1,0:T(8,128)(2,1)S(1)} all-gather(bf16[24,512]{1,0:T(8,128)(2,1)S(1)} %copy-done.63), channel_id=1, replica_groups=mesh['fsdp'=32] {'fsdp'}, dimensions={0}, use_global_device_ids=true | all-gather | bytes 811008 | tf_op jit(solution)/shard_map/all_gather | solution.py:349
  176.5 19.8 %all-gather.12.cloned.1.call-done = bf16[768,3072]{1,0:T(8,128)(2,1)} async-done(((bf16[24,3072]{1,0:T(8,128)(2,1)}), bf16[768,3072]{1,0:T(8,128)(2,1)}) %all-gather.12.cloned.1.call-update) | async-done | bytes 4718608 | tf_op jit(solution)/shard_map/all_gather | solution.py:342
  196.2 15.7 multiply_convert_fusion.2
  212.0 49.5 %all-gather.14.cloned.1.call-done = bf16[3072,768]{1,0:T(8,128)(2,1)} async-done(((bf16[96,768]{1,0:T(8,128)(2,1)}), bf16[3072,768]{1,0:T(8,128)(2,1)}) %all-gather.14.cloned.1.call-update) | async-done | bytes 4718608 | tf_op jit(solution)/shard_map/all_gather | solution.py:344
  271.9 46.0 %all-gather.16.cloned.1.call-done = bf16[512,1536]{1,0:T(8,128)(2,1)} async-done(((bf16[16,1536]{1,0:T(8,128)(2,1)}), bf16[512,1536]{1,0:T(8,128)(2,1)}) %all-gather.16.cloned.1.call-update) | async-done | bytes 1572880 | tf_op jit(solution)/shard_map/all_gather | solution.py:354
  338.4 10.4 fusion.72
  350.0 26.0 %all-gather.18.cloned.1.call-done = bf16[512,2048]{1,0:T(8,128)(2,1)} async-done(((bf16[16,2048]{1,0:T(8,128)(2,1)}), bf16[512,2048]{1,0:T(8,128)(2,1)}) %all-gather.18.cloned.1.call-update) | async-done | bytes 2097168 | tf_op jit(solution)/shard_map/all_gather | solution.py:361
  381.1 53.0 %all-gather.20.cloned.1.call-done = bf16[2048,512]{1,0:T(8,128)(2,1)} async-done(((bf16[64,512]{1,0:T(8,128)(2,1)}), bf16[2048,512]{1,0:T(8,128)(2,1)}) %all-gather.20.cloned.1.call-update) | async-done | bytes 2097168 | tf_op jit(solution)/shard_map/all_gather | solution.py:363
  434.1 14.9 fusion.158
  456.0 12.2 fusion.177
  468.2 10.7 fusion.165
  478.9 30.5 %fusion.69 = bf16[16,32,529]{2,1,0:T(8,128)(2,1)} fusion(bf16[529,16,32]{0,2,1:T(8,128)(2,1)} %bitcast.109, f32[16,529,529]{1,2,0:T(8,128)} %fusion.177, f32[16,529]{1,0:T(8,128)S(1)} %log_add_fusion, f32[16,529,529]{1,2,0:T(8,128)} %copy-done, pred[529,529]{0,1:T(8,128)(4,1)S(1)} %copy-done.20), kind=kOutput, calls=%fused_computation.97 | convolution fusion | flops 336089024 | bytes 37216736 | tf_op jit(solution)/shard_map/bhqk,bqhd->bkhd/dot_general | solution.py:93
  509.4 39.2 %fusion.166 = (f32[16,32]{1,0:T(8,128)S(1)}, bf16[1,529,16,32]{1,3,2,0:T(8,128)(2,1)}) fusion(bf16[529,16,32]{0,2,1:T(8,128)(2,1)S(1)} %bitcast.107, f32[16,529,529]{1,2,0:T(8,128)} %fusion.177, f32[16,529]{1,0:T(8,128)S(1)} %log_add_fusion, f32[16,529,529]{1,2,0:T(8,128)} %copy-done, pred[529,529]{0,1:T(8,128)(4,1)S(1)} %copy-done.20), kind=kOutput, calls=%fused_computation.234 | convolution fusion | flops 336359360 | bytes 37218784 | tf_op jit(solution)/shard_map/bhqk,bkhd->bqhd/dot_general | solution.py:90
  562.4 9.0 fusion.176
  571.4 6.1 multiply_reduce_fusion.2
  593.0 13.4 fusion.78
  606.5 13.3 fusion.168
  659.5 6.2 fusion.102
  667.1 7.2 fusion.90
  675.5 8.0 fusion.107
  690.9 86.9 %all-reduce.45.cloned.1.call-done = (f32[768]{0:T(1024)}, f32[768]{0:T(1024)}, f32[768]{0:T(1024)}, f32[768]{0:T(1024)}, f32[768]{0:T(1024)}, /*index=5*/f32[768...) async-done(((f32[768]{0:T(1024)}, f32[768]{0:T(1024)}, ...) | async-done | bytes 65552
  802.8 115.0 %reduce-scatter.22.cloned.1.call-done = f32[16,512]{1,0:T(8,128)} async-done(((f32[512,512]{1,0:T(8,128)}), f32[16,512]{1,0:T(8,128)}) %reduce-scatter.22.cloned.1.call-update) | async-done | bytes 32784 | tf_op jit(solution)/shard_map/reduce_scatter | solution.py:420
  917.9 99.5 %reduce-scatter.18.cloned.1.call-done = f32[24,512]{1,0:T(8,128)} async-done(((f32[768,512]{1,0:T(8,128)}), f32[24,512]{1,0:T(8,128)}) %reduce-scatter.18.cloned.1.call-update) | async-done | bytes 49168 | tf_op jit(solution)/shard_map/reduce_scatter | solution.py:412
  1017.3 104.8 %reduce-scatter.12.cloned.1.call-done = f32[24,768]{1,0:T(8,128)} async-done(((f32[768,768]{1,0:T(8,128)}), f32[24,768]{1,0:T(8,128)}) %reduce-scatter.12.cloned.1.call-update) | async-done | bytes 73744 | tf_op jit(solution)/shard_map/reduce_scatter | solution.py:451
  1122.1 106.4 %reduce-scatter.20.cloned.1.call-done = f32[16,1536]{1,0:T(8,128)} async-done(((f32[512,1536]{1,0:T(8,128)}), f32[16,1536]{1,0:T(8,128)}) %reduce-scatter.20.cloned.1.call-update) | async-done | bytes 98320 | tf_op jit(solution)/shard_map/reduce_scatter | solution.py:417
  1228.5 142.8 %reduce-scatter.24.cloned.1.call-done = f32[16,2048]{1,0:T(8,128)} async-done(((f32[512,2048]{1,0:T(8,128)}), f32[16,2048]{1,0:T(8,128)}) %reduce-scatter.24.cloned.1.call-update) | async-done | bytes 131088 | tf_op jit(solution)/shard_map/reduce_scatter | solution.py:424
  1371.3 139.3 %reduce-scatter.26.cloned.1.call-done = f32[64,512]{1,0:T(8,128)} async-done(((f32[2048,512]{1,0:T(8,128)}), f32[64,512]{1,0:T(8,128)}) %reduce-scatter.26.cloned.1.call-update) | async-done | bytes 131088 | tf_op jit(solution)/shard_map/reduce_scatter | solution.py:426
  1510.7 121.3 %reduce-scatter.10.cloned.1.call-done = f32[24,2304]{1,0:T(8,128)} async-done(((f32[768,2304]{1,0:T(8,128)}), f32[24,2304]{1,0:T(8,128)}) %reduce-scatter.10.cloned.1.call-update) | async-done | bytes 221200 | tf_op jit(solution)/shard_map/reduce_scatter | solution.py:448
  1632.0 142.2 %reduce-scatter.14.cloned.1.call-done = f32[24,3072]{1,0:T(8,128)} async-done(((f32[768,3072]{1,0:T(8,128)}), f32[24,3072]{1,0:T(8,128)}) %reduce-scatter.14.cloned.1.call-update) | async-done | bytes 294928 | tf_op jit(solution)/shard_map/reduce_scatter | solution.py:455
  1774.2 140.9 %reduce-scatter.16.cloned.1.call-done = f32[96,768]{1,0:T(8,128)} async-done(((f32[3072,768]{1,0:T(8,128)}), f32[96,768]{1,0:T(8,128)}) %reduce-scatter.16.cloned.1.call-update) | async-done | bytes 294928 | tf_op jit(solution)/shard_map/reduce_scatter | solution.py:457
  (414 shorter events, 191.3 us)
Async XLA Ops:
  7.4 67.3 %copy-start.71 = (bf16[16,512]{1,0:T(8,128)(2,1)S(1)}, bf16[16,512]{1,0:T(8,128)(2,1)}, u32[]{:S(2)}) copy-start(bf16[16,512]{1,0:T(8,128)(2,1)} %param.58) | copy-start | bytes 49156
  7.4 109.5 %copy-start.63 = (bf16[24,512]{1,0:T(8,128)(2,1)S(1)}, bf16[24,512]{1,0:T(8,128)(2,1)}, u32[]{:S(2)}) copy-start(bf16[24,512]{1,0:T(8,128)(2,1)} %param.50) | copy-start | bytes 73732
  7.5 148.8 %all-gather.8.cloned.1.call-start = ((), (), s32[]{:S(2)}) async-start(), calls=%async_computation.9 | async-start | bytes 3649536 | tf_op jit(solution)/shard_map/all_gather | solution.py:335
  8.2 165.8 %all-gather.10.cloned.1.call-start = ((), (), s32[]{:S(2)}) async-start(), calls=%async_computation.10 | async-start | bytes 1216512 | tf_op jit(solution)/shard_map/all_gather | solution.py:338
  8.9 187.3 %all-gather.12.cloned.1.call-start = ((), (), s32[]{:S(2)}) async-start(), calls=%async_computation.11 | async-start | bytes 4866048 | tf_op jit(solution)/shard_map/all_gather | solution.py:342
  9.7 251.8 %all-gather.14.cloned.1.call-start = ((), (), s32[]{:S(2)}) async-start(), calls=%async_computation.12 | async-start | bytes 4866048 | tf_op jit(solution)/shard_map/all_gather | solution.py:344
  10.2 307.7 %all-gather.16.cloned.1.call-start = ((), (), s32[]{:S(2)}) async-start(), calls=%async_computation.13 | async-start | bytes 1622016 | tf_op jit(solution)/shard_map/all_gather | solution.py:354
  10.8 365.2 %all-gather.18.cloned.1.call-start = ((), (), s32[]{:S(2)}) async-start(), calls=%async_computation.14 | async-start | bytes 2162688 | tf_op jit(solution)/shard_map/all_gather | solution.py:361
  11.4 422.7 %all-gather.20.cloned.1.call-start = ((), (), s32[]{:S(2)}) async-start(), calls=%async_computation.15 | async-start | bytes 2162688 | tf_op jit(solution)/shard_map/all_gather | solution.py:363
  12.2 765.6 %all-reduce.45.cloned.1.call-start = ((), (), s32[]{:S(2)}) async-start(), calls=%async_computation.25 | async-start | bytes 147456
  14.5 323.9 %copy-start.19 = (pred[529,529]{0,1:T(8,128)(4,1)}, pred[529,529]{0,1:T(8,128)(4,1)S(1)}, u32[]{:S(2)}) copy-start(pred[529,529]{0,1:T(8,128)(4,1)S(1)} %broadcast_compare_fusion) | copy-start | bytes 839527
  19.9 140.5 %copy-start.46 = (f32[384]{0:T(512)}, f32[384]{0:T(512)S(1)}, u32[]{:S(2)}) copy-start(f32[384]{0:T(512)S(1)} %broadcast_multiply_fusion.3) | copy-start | bytes 4612
  20.2 140.2 %copy-start.52 = (f32[384]{0:T(512)}, f32[384]{0:T(512)S(1)}, u32[]{:S(2)}) copy-start(f32[384]{0:T(512)S(1)} %fusion.125) | copy-start | bytes 4612
  72.0 246.0 %copy-start.72 = (f32[512]{0:T(512)}, f32[512]{0:T(512)S(1)}, u32[]{:S(2)}) copy-start(f32[512]{0:T(512)S(1)} %convert_element_type.209) | copy-start | bytes 6148
  73.8 86.6 %copy-start.42 = (f32[768]{0:T(1024)}, f32[768]{0:T(1024)S(1)}, u32[]{:S(2)}) copy-start(f32[768]{0:T(1024)S(1)} %convert_element_type.188) | copy-start | bytes 9220
  73.8 122.4 %copy-start.44 = (f32[768]{0:T(1024)}, f32[768]{0:T(1024)S(1)}, u32[]{:S(2)}) copy-start(f32[768]{0:T(1024)S(1)} %convert_element_type.201) | copy-start | bytes 9220
  73.8 86.6 %copy-start.50 = (f32[768]{0:T(1024)}, f32[768]{0:T(1024)S(1)}, u32[]{:S(2)}) copy-start(f32[768]{0:T(1024)S(1)} %convert_element_type.189) | copy-start | bytes 9220
  73.9 122.4 %copy-start.48 = (f32[768]{0:T(1024)}, f32[768]{0:T(1024)S(1)}, u32[]{:S(2)}) copy-start(f32[768]{0:T(1024)S(1)} %convert_element_type.202) | copy-start | bytes 9220
  117.0 231.9 %copy-start.16 = (bf16[512,512]{1,0:T(8,128)(2,1)}, bf16[512,512]{1,0:T(8,128)(2,1)S(1)}, u32[]{:S(2)}) copy-start(bf16[512,512]{1,0:T(8,128)(2,1)S(1)} %all_gather.121) | copy-start | bytes 1572868
  156.3 110.3 %copy-start.18 = (bf16[768,512]{1,0:T(8,128)(2,1)}, bf16[768,512]{1,0:T(8,128)(2,1)S(1)}, u32[]{:S(2)}) copy-start(bf16[768,512]{1,0:T(8,128)(2,1)S(1)} %all_gather.114) | copy-start | bytes 2359300
  176.1 85.4 %copy-start.8 = (f32[384,768]{1,0:T(8,128)}, f32[384,768]{1,0:T(8,128)S(1)}, u32[]{:S(2)}) copy-start(f32[384,768]{1,0:T(8,128)S(1)} %get-tuple-element.120) | copy-start | bytes 3538948
  349.7 101.5 %copy-start.11 = (f32[529,512]{1,0:T(8,128)}, f32[529,512]{1,0:T(8,128)S(1)}, u32[]{:S(2)}) copy-start(f32[529,512]{1,0:T(8,128)S(1)} %get-tuple-element.125) | copy-start | bytes 3250180
  350.0 84.1 %copy-start.39 = (bf16[529,512]{1,0:T(8,128)(2,1)S(1)}, bf16[529,512]{1,0:T(8,128)(2,1)}, u32[]{:S(2)}) copy-start(bf16[529,512]{1,0:T(8,128)(2,1)} %param.36) | copy-start | bytes 1625092
  628.9 289.0 %reduce-scatter.22.cloned.1.call-start = ((), (), s32[]{:S(2)}) async-start(), calls=%async_computation.22 | async-start | bytes 1081344 | tf_op jit(solution)/shard_map/reduce_scatter | solution.py:420
  631.6 385.7 %reduce-scatter.18.cloned.1.call-start = ((), (), s32[]{:S(2)}) async-start(), calls=%async_computation.20 | async-start | bytes 1622016 | tf_op jit(solution)/shard_map/reduce_scatter | solution.py:412
  634.8 487.3 %reduce-scatter.12.cloned.1.call-start = ((), (), s32[]{:S(2)}) async-start(), calls=%async_computation.17 | async-start | bytes 2433024 | tf_op jit(solution)/shard_map/reduce_scatter | solution.py:451
  637.3 591.2 %reduce-scatter.20.cloned.1.call-start = ((), (), s32[]{:S(2)}) async-start(), calls=%async_computation.21 | async-start | bytes 3244032 | tf_op jit(solution)/shard_map/reduce_scatter | solution.py:417
  642.4 729.0 %reduce-scatter.24.cloned.1.call-start = ((), (), s32[]{:S(2)}) async-start(), calls=%async_computation.23 | async-start | bytes 4325376 | tf_op jit(solution)/shard_map/reduce_scatter | solution.py:424
  648.1 862.5 %reduce-scatter.26.cloned.1.call-start = ((), (), s32[]{:S(2)}) async-start(), calls=%async_computation.24 | async-start | bytes 4325376 | tf_op jit(solution)/shard_map/reduce_scatter | solution.py:426
  658.1 973.8 %reduce-scatter.10.cloned.1.call-start = ((), (), s32[]{:S(2)}) async-start(), calls=%async_computation.16 | async-start | bytes 7299072 | tf_op jit(solution)/shard_map/reduce_scatter | solution.py:448
  665.8 1108.4 %reduce-scatter.14.cloned.1.call-start = ((), (), s32[]{:S(2)}) async-start(), calls=%async_computation.18 | async-start | bytes 9732096 | tf_op jit(solution)/shard_map/reduce_scatter | solution.py:455
  674.3 1240.8 %reduce-scatter.16.cloned.1.call-start = ((), (), s32[]{:S(2)}) async-start(), calls=%async_computation.19 | async-start | bytes 9732096 | tf_op jit(solution)/shard_map/reduce_scatter | solution.py:457
  (88 other events, 1205.0 us)
Sparse Core Ops, SparseCore 0:
  11.2 63.1 all-gather.7
  77.2 53.4 all-gather.9
  133.6 62.5 all-gather.11
  199.0 62.4 all-gather.13
  264.2 53.7 all-gather.15
  320.7 55.2 all-gather.17
  378.8 55.2 all-gather.19
  629.0 148.6 all-reduce.44
  780.6 137.2 reduce-scatter.21
  924.4 92.9 reduce-scatter.17
  1024.0 98.0 reduce-scatter.11
  1128.0 100.4 reduce-scatter.19
  1231.4 139.9 reduce-scatter.23
  1374.0 136.5 reduce-scatter.25
  1516.8 115.1 reduce-scatter.9
  1639.3 134.8 reduce-scatter.13
  1780.5 134.4 reduce-scatter.15
where the time goes:
time: 1930 us; the launch traced here: 1920 us
  waiting for transfers between devices  1400 us (73%)
  matrix products  279 us (14%)
  blocking collectives  125 us (6%)
  local copies, waits for them, and re-layouts  70.3 us (4%)
  other arithmetic  33.1 us (2%)
    reduce_scatter x1, waiting for transfers between devices, on_device(): lax.psum_scatter(dec_grads[9], 'fsdp', scatter_dimension=0, tiled=True)  143 us
    reduce_scatter x1, waiting for transfers between devices, on_device(): lax.psum_scatter(enc_grads[9], 'fsdp', scatter_dimension=0, tiled=True)  142 us
    reduce_scatter x1, waiting for transfers between devices, on_device(): lax.psum_scatter(enc_grads[11], 'fsdp', scatter_dimension=0, tiled=True)  141 us
    reduce_scatter x1, waiting for transfers between devices, on_device(): lax.psum_scatter(dec_grads[11], 'fsdp', scatter_dimension=0, tiled=True)  139 us
    reduce_scatter x1, waiting for transfers between devices, on_device(): lax.psum_scatter(enc_grads[2], 'fsdp', scatter_dimension=0, tiled=True)  121 us
    reduce_scatter x1, waiting for transfers between devices, on_device(): lax.psum_scatter(dec_grads[5], 'fsdp', scatter_dimension=0, tiled=True)  115 us
    reduce_scatter x1, waiting for transfers between devices, on_device(): lax.psum_scatter(dec_grads[2], 'fsdp', scatter_dimension=0, tiled=True)  106 us
    reduce_scatter x1, waiting for transfers between devices, on_device(): lax.psum_scatter(enc_grads[5], 'fsdp', scatter_dimension=0, tiled=True)  105 us
  transfers between devices with their start and end apart: 17, of which 15 were waited for; matrix products, arithmetic and copies ran while one was open for 9% of the time, Pallas kernels for 0%

commit v1 on v0

--- a/solution.py
+++ b/solution.py
@@ -1,6 +1,8 @@
 import jax
 import jax.numpy as jnp
 from jax import lax
+from jax.experimental import pallas as pl
+from jax.experimental.pallas import tpu as pltpu
 from jax.sharding import PartitionSpec as P
 
 HEADS = 12
@@ -190,14 +192,14 @@
     ) = saved
     grad_low = grad_out.astype(jnp.bfloat16)
     grad_down_bias = jnp.sum(grad_out, 0)
-    grad_down = jnp.einsum("rf,rw->fw", activated, grad_low, preferred_element_type=jnp.float32)
+    grad_down = jnp.einsum("rf,rw->fw", activated, grad_low, preferred_element_type=jnp.float32).astype(jnp.bfloat16)
     grad_act = jnp.einsum("rw,fw->rf", grad_low, w_down, preferred_element_type=jnp.float32)
     grad_hidden = jax.vjp(gelu_exact, hidden_up)[1](grad_act)[0]
     grad_hidden_low = grad_hidden.astype(jnp.bfloat16)
     grad_up_bias = jnp.sum(grad_hidden, 0)
     grad_up = jnp.einsum(
         "rd,rf->df", normed_two, grad_hidden_low, preferred_element_type=jnp.float32
-    )
+    ).astype(jnp.bfloat16)
     grad_normed_two = jnp.einsum(
         "rf,df->rd", grad_hidden_low, w_up, preferred_element_type=jnp.float32
     )
@@ -247,7 +249,7 @@
     grad_out_bias = jnp.sum(grad_middle, 0)
     grad_w_out = jnp.einsum(
         "rv,rw->vw", attended, grad_middle_low, preferred_element_type=jnp.float32
-    )
+    ).astype(jnp.bfloat16)
     grad_attended = jnp.einsum(
         "rw,vw->rv", grad_middle_low, w_out, preferred_element_type=jnp.float32
     ).astype(jnp.bfloat16)
@@ -266,7 +268,7 @@
     grad_query_bias = jnp.sum(grad_query, 0)
     grad_value_bias = jnp.sum(grad_value, 0)
     grad_joined = jnp.concatenate([grad_query, grad_key, grad_value], 1).astype(jnp.bfloat16)
-    grad_qkv = jnp.einsum("rd,rc->dc", normed, grad_joined, preferred_element_type=jnp.float32)
+    grad_qkv = jnp.einsum("rd,rc->dc", normed, grad_joined, preferred_element_type=jnp.float32).astype(jnp.bfloat16)
     grad_normed = jnp.einsum("rc,dc->rd", grad_joined, w_qkv, preferred_element_type=jnp.float32)
     grad_in_norm, grad_gain_one, grad_shift_one = norm_back(
         stream, widen(gain_one), widen(shift_one), grad_normed
@@ -287,6 +289,412 @@
     grad_middle, feed_grads = back_feed(grad_out, params, saved)
     grad_in, attend_grads = back_attend(grad_middle, params, seg_ids, head_count, saved)
     return (grad_in, attend_grads + feed_grads)
+
+
+MESH = pl.DeviceIdType.MESH
+VMEM_BYTES = 60 * 2**20
+
+
+class Place:
+    def __init__(self):
+        me = lax.axis_index("fsdp")
+        self.c = c = lax.rem(me, 2)
+        x = lax.rem(me // 2, 2)
+        y = lax.rem(me // 4, 2)
+        self.z0 = lax.rem(me // 8, 2)
+        self.z1 = lax.rem(me // 16, 2)
+        self.stride1 = 1 + c
+        self.stride2 = 2 - c
+        self.bit1 = x * (1 - c) + y * c
+        self.bit2 = y * (1 - c) + x * c
+        self.here = 2 * y + x
+        self.core = me + 1 - 2 * c
+        self.first = me + 2 * self.stride1 * (1 - 2 * self.bit1)
+        self.second = me + 2 * self.stride2 * (1 - 2 * self.bit2)
+        self.near = me + 8 * (1 - 2 * self.z0)
+        self.far = me + 16 * (1 - 2 * self.z1)
+
+    def along_second(self, bit1, j):
+        return bit1 * self.stride1 + j * self.stride2
+
+    def barrier(self):
+        barrier = pltpu.get_barrier_semaphore()
+        for partner in (self.core, self.first, self.second, self.near, self.far):
+            pl.semaphore_signal(barrier, inc=1, device_id=(partner,), device_id_type=MESH)
+        pl.semaphore_wait(barrier, 5)
+
+
+def padded(rows):
+    return -(-rows // 16) * 16
+
+
+def gather_kernel(shapes, *refs):
+    count = len(shapes)
+    shards, vec_ref = refs[:count], refs[count]
+    wholes, vec_out = refs[count + 1 : 2 * count + 1], refs[2 * count + 1]
+    scratch = refs[2 * count + 2 :]
+    sent, got, tiles = scratch[:count], scratch[count : 2 * count], scratch[2 * count : 3 * count]
+    send_sem, recv_sem, local_sem = scratch[3 * count :]
+    at = Place()
+    at.barrier()
+    started = []
+
+    def send(src, dst, m, k, partner):
+        copy = pltpu.make_async_remote_copy(
+            src_ref=src,
+            dst_ref=dst,
+            send_sem=send_sem.at[m, k],
+            recv_sem=recv_sem.at[m, k],
+            device_id=(partner,),
+            device_id_type=MESH,
+        )
+        copy.start()
+        started.append(copy)
+        return copy
+
+    def view(m, z1, z0, yx):
+        if m == count:
+            return vec_out.at[z1, z0, yx, at.c]
+        rows, columns = shapes[m]
+        half = columns // 2
+        lanes = pl.ds(pl.multiple_of(at.c * half, 128), half)
+        if yx is None:
+            return wholes[m].at[z1, z0, :, lanes]
+        return wholes[m].at[z1, z0, pl.ds(pl.multiple_of(yx * 2 * rows, 16), 2 * rows), lanes]
+
+    def my_half(m, mine):
+        half = shapes[m][1] // 2
+        low, high = shards[m][:, :half].astype(jnp.float32), shards[m][:, half:].astype(jnp.float32)
+        return jnp.where(at.c == 0, low, high) if mine else jnp.where(at.c == 0, high, low)
+
+    every = slice(None)
+    flights = {}
+
+    def stage(m, k):
+        if k == 0:
+            if m == count:
+                return
+            rows, columns = shapes[m]
+            value = my_half(m, False)
+            extra = padded(rows) - rows
+            if extra:
+                value = jnp.concatenate([value, jnp.zeros((extra, columns // 2), jnp.float32)], 0)
+            sent[m][...] = value.astype(jnp.bfloat16)
+            flights[m, 0] = [send(sent[m], got[m], m, 0, at.core)]
+        elif k == 1:
+            if m == count:
+                local = pltpu.make_async_copy(vec_ref, view(m, at.z1, at.z0, at.here), local_sem.at[m])
+                local.start()
+                flights[m, 1] = [send(vec_ref, view(m, at.z1, at.z0, at.here), m, 1, at.far)]
+            else:
+                rows = shapes[m][0]
+                flights[m, 0][0].wait_recv()
+                other = got[m][...].astype(jnp.float32)[:rows]
+                mine = my_half(m, True)
+                both = jnp.concatenate(
+                    [jnp.where(at.c == 0, mine, other), jnp.where(at.c == 0, other, mine)], 0
+                )
+                tiles[m][...] = both.astype(jnp.bfloat16)
+                local = pltpu.make_async_copy(tiles[m], view(m, at.z1, at.z0, at.here), local_sem.at[m])
+                local.start()
+                flights[m, 1] = [send(tiles[m], view(m, at.z1, at.z0, at.here), m, 1, at.far)]
+            flights[m, "local"] = local
+        elif k == 2:
+            flights[m, "local"].wait()
+            flights[m, 1][0].wait_recv()
+            part = view(m, every, at.z0, at.here)
+            flights[m, 2] = [send(part, part, m, 2, at.near)]
+        elif k == 3:
+            flights[m, 2][0].wait_recv()
+            part = view(m, every, every, at.here)
+            flights[m, 3] = [send(part, part, m, 3, at.second)]
+        elif k == 4:
+            flights[m, 3][0].wait_recv()
+            flights[m, 4] = []
+            for j in range(2):
+                part = view(m, every, every, at.along_second(at.bit1, j))
+                flights[m, 4].append(send(part, part, m, 4 + j, at.first))
+        elif k == 5:
+            for copy in flights[m, 4]:
+                copy.wait_recv()
+            part = vec_out.at[:, :, :, at.c] if m == count else view(m, every, every, None)
+            flights[m, 5] = [send(part, part, m, 6, at.core)]
+        else:
+            flights[m, 5][0].wait_recv()
+
+    order = [count] + list(range(count))
+    for step in range(len(order) + 6):
+        for k in range(6, -1, -1):
+            if 0 <= step - k < len(order):
+                stage(order[step - k], k)
+    for copy in started:
+        copy.wait_send()
+
+
+def gather_all(shards, vec):
+    shapes = [shard.shape for shard in shards]
+    count = len(shapes)
+    any_space = pl.BlockSpec(memory_space=pl.ANY)
+    vmem = pl.BlockSpec(memory_space=pltpu.VMEM)
+    out_shape = [jax.ShapeDtypeStruct((2, 2, 8 * r, c), jnp.bfloat16) for r, c in shapes]
+    out_shape.append(jax.ShapeDtypeStruct((2, 2, 4, 2, 8, 128), jnp.float32))
+    scratch = [pltpu.VMEM((padded(r), c // 2), jnp.bfloat16) for r, c in shapes] * 2
+    scratch += [pltpu.VMEM((2 * r, c // 2), jnp.bfloat16) for r, c in shapes]
+    scratch += [
+        pltpu.SemaphoreType.DMA((count + 1, 7)),
+        pltpu.SemaphoreType.DMA((count + 1, 7)),
+        pltpu.SemaphoreType.DMA((count + 1,)),
+    ]
+
+    def body(*refs):
+        gather_kernel(shapes, *refs)
+
+    return pl.pallas_call(
+        body,
+        out_shape=out_shape,
+        in_specs=[vmem] * (count + 1),
+        out_specs=[any_space] * (count + 1),
+        scratch_shapes=scratch,
+        compiler_params=pltpu.CompilerParams(
+            collective_id=0, has_side_effects=True, vmem_limit_bytes=VMEM_BYTES
+        ),
+        name="gather_params",
+    )(*shards, vec)
+
+
+def add_rows(dst, src, rows):
+    def body(i, carry):
+        part = pl.ds(pl.multiple_of(i * 16, 16), 16)
+        dst[part, :] = (dst[part, :].astype(jnp.float32) + src[part, :].astype(jnp.float32)).astype(dst.dtype)
+        return carry
+
+    lax.fori_loop(0, rows // 16, body, 0)
+
+
+def scatter_kernel(shapes, *refs):
+    count = len(shapes)
+    grads, vec_ref = refs[:count], refs[count]
+    outs, vec_out = refs[count + 1 : 2 * count + 1], refs[2 * count + 1]
+    scratch = list(refs[2 * count + 2 :])
+    groups = [scratch[i * count : (i + 1) * count] for i in range(8)]
+    acc, got0, got1, got2, got3, got4, final, got5 = groups
+    vec_acc, vgot0, vgot1, vgot2, vgot3, vgot4, send_sem, recv_sem, local_sem = scratch[8 * count :]
+    at = Place()
+    at.barrier()
+    started = []
+
+    def send(src, dst, m, k, partner):
+        copy = pltpu.make_async_remote_copy(
+            src_ref=src,
+            dst_ref=dst,
+            send_sem=send_sem.at[m, k],
+            recv_sem=recv_sem.at[m, k],
+            device_id=(partner,),
+            device_id_type=MESH,
+        )
+        copy.start()
+        started.append(copy)
+        return copy
+
+    def lanes(m, core):
+        half = shapes[m][1] // 2
+        return pl.ds(pl.multiple_of(core * half, 128), half)
+
+    def block(m, z1, z0, yx):
+        if m == count:
+            return vec_acc.at[z1, z0, yx]
+        rows = 2 * shapes[m][0]
+        return acc[m].at[z1, z0, pl.ds(pl.multiple_of(yx * rows, 16), rows)]
+
+    every = slice(None)
+    flights = {}
+    got = {
+        1: lambda m: vgot1 if m == count else got1[m],
+        2: lambda m: vgot2 if m == count else got2[m],
+        3: lambda m: vgot3 if m == count else got3[m],
+        4: lambda m: vgot4 if m == count else got4[m],
+    }
+
+    def add(m, dst, src):
+        if m == count:
+            dst[...] += src[...]
+        else:
+            add_rows(dst, src, dst.shape[0])
+
+    def finish(m, k):
+        for copy in flights[m, k]:
+            copy.wait_recv()
+        if k == 0:
+            flights[m, "local"].wait()
+            if m == count:
+                vec_acc[...] += vgot0[...]
+            else:
+                for z1 in range(2):
+                    for z0 in range(2):
+                        add_rows(acc[m].at[z1, z0], got0[m].at[z1, z0], 8 * shapes[m][0])
+        elif k == 1:
+            for j in range(2):
+                for z1 in range(2):
+                    for z0 in range(2):
+                        add(m, block(m, z1, z0, at.along_second(at.bit1, j)), got[1](m).at[j, z1, z0])
+        elif k == 2:
+            for z1 in range(2):
+                for z0 in range(2):
+                    add(m, block(m, z1, z0, at.here), got[2](m).at[z1, z0])
+        elif k == 3:
+            for z1 in range(2):
+                add(m, block(m, z1, at.z0, at.here), got[3](m).at[z1])
+        elif k == 4:
+            mine = block(m, at.z1, at.z0, at.here)
+            if m == count:
+                vec_out[...] = mine[...] + vgot4[...]
+            else:
+                rows = shapes[m][0]
+                total = mine[...].astype(jnp.float32) + got4[m][...].astype(jnp.float32)
+                final[m][0] = total[:rows]
+                final[m][1] = total[rows:]
+        elif m < count:
+            half = shapes[m][1] // 2
+            for core in range(2):
+
+                @pl.when(at.c == core)
+                def _():
+                    outs[m][:, core * half : (core + 1) * half] = final[m][core]
+                    outs[m][:, (1 - core) * half : (2 - core) * half] = got5[m][...]
+
+    def start(m, k):
+        if k == 0:
+            if m == count:
+                local = pltpu.make_async_copy(vec_ref.at[:, :, :, at.c], vec_acc, local_sem.at[m])
+                local.start()
+                flights[m, 0] = [send(vec_ref.at[:, :, :, 1 - at.c], vgot0, m, 0, at.core)]
+            else:
+                flights[m, 0] = [send(grads[m].at[:, :, :, lanes(m, 1 - at.c)], got0[m], m, 0, at.core)]
+                local = pltpu.make_async_copy(grads[m].at[:, :, :, lanes(m, at.c)], acc[m], local_sem.at[m])
+                local.start()
+            flights[m, "local"] = local
+        elif k == 1:
+            flights[m, 1] = [
+                send(
+                    block(m, every, every, at.along_second(1 - at.bit1, j)),
+                    got[1](m).at[j],
+                    m,
+                    1 + j,
+                    at.first,
+                )
+                for j in range(2)
+            ]
+        elif k == 2:
+            away = at.along_second(at.bit1, 1 - at.bit2)
+            flights[m, 2] = [send(block(m, every, every, away), got[2](m), m, 3, at.second)]
+        elif k == 3:
+            flights[m, 3] = [send(block(m, every, 1 - at.z0, at.here), got[3](m), m, 4, at.near)]
+        elif k == 4:
+            flights[m, 4] = [send(block(m, 1 - at.z1, at.z0, at.here), got[4](m), m, 5, at.far)]
+        else:
+            flights[m, 5] = [] if m == count else [send(final[m].at[1 - at.c], got5[m], m, 6, at.core)]
+
+    order = list(range(count)) + [count]
+    for step in range(len(order) + 6):
+        for k in range(6, -1, -1):
+            if 0 <= step - k < len(order):
+                m = order[step - k]
+                if k > 0:
+                    finish(m, k - 1)
+                if k < 6:
+                    start(m, k)
+    for copy in started:
+        copy.wait_send()
+
+
+def scatter_all(grads, vec):
+    shapes = [(g.shape[2] // 8, g.shape[3]) for g in grads]
+    count = len(shapes)
+    any_space = pl.BlockSpec(memory_space=pl.ANY)
+    vmem = pl.BlockSpec(memory_space=pltpu.VMEM)
+    bf16, f32 = jnp.bfloat16, jnp.float32
+    scratch = [pltpu.VMEM((2, 2, 8 * r, c // 2), bf16) for r, c in shapes] * 2
+    scratch += [pltpu.VMEM((2, 2, 2, 2 * r, c // 2), bf16) for r, c in shapes]
+    scratch += [pltpu.VMEM((2, 2, 2 * r, c // 2), bf16) for r, c in shapes]
+    scratch += [pltpu.VMEM((2, 2 * r, c // 2), bf16) for r, c in shapes]
+    scratch += [pltpu.VMEM((2 * r, c // 2), bf16) for r, c in shapes]
+    scratch += [pltpu.VMEM((2, r, c // 2), f32) for r, c in shapes]
+    scratch += [pltpu.VMEM((r, c // 2), f32) for r, c in shapes]
+    scratch += [
+        pltpu.VMEM((2, 2, 4, 8, 128), f32),
+        pltpu.VMEM((2, 2, 4, 8, 128), f32),
+        pltpu.VMEM((2, 2, 2, 8, 128), f32),
+        pltpu.VMEM((2, 2, 8, 128), f32),
+        pltpu.VMEM((2, 8, 128), f32),
+        pltpu.VMEM((8, 128), f32),
+        pltpu.SemaphoreType.DMA((count + 1, 7)),
+        pltpu.SemaphoreType.DMA((count + 1, 7)),
+        pltpu.SemaphoreType.DMA((count + 1,)),
+    ]
+    out_shape = [jax.ShapeDtypeStruct((r, c), f32) for r, c in shapes]
+    out_shape.append(jax.ShapeDtypeStruct((8, 128), f32))
+
+    def body(*refs):
+        scatter_kernel(shapes, *refs)
+
+    return pl.pallas_call(
+        body,
+        out_shape=out_shape,
+        in_specs=[any_space] * (count + 1),
+        out_specs=[vmem] * (count + 1),
+        scratch_shapes=scratch,
+        compiler_params=pltpu.CompilerParams(
+            collective_id=1, has_side_effects=True, vmem_limit_bytes=VMEM_BYTES
+        ),
+        name="scatter_grads",
+    )(*grads, vec)
+
+
+def on_links(matrices, vectors):
+    values = sum(v.shape[0] for v in vectors)
+    return (
+        lax.axis_size("fsdp") == 32
+        and values <= 1024
+        and all(m.shape[0] % 8 == 0 and m.shape[1] % 256 == 0 for m in matrices)
+    )
+
+
+def split_vectors(joined, sizes):
+    pieces, start = [], 0
+    for size in sizes:
+        pieces.append(joined[:, start : start + size].reshape(-1))
+        start += size
+    return pieces
+
+
+def gather_params(matrices, vectors):
+    sizes = [v.shape[0] for v in vectors]
+    joined = jnp.concatenate(vectors).astype(jnp.float32)
+    if on_links(matrices, vectors):
+        tile = jnp.pad(joined, (0, 1024 - joined.shape[0])).reshape(8, 128)
+        *whole, whole_vec = gather_all(matrices, tile)
+        whole = [w.reshape(-1, w.shape[3]) for w in whole]
+        return whole, split_vectors(whole_vec.reshape(32, 1024), sizes)
+    whole = [lax.all_gather(m, "fsdp", axis=0, tiled=True) for m in matrices]
+    return whole, split_vectors(lax.all_gather(joined, "fsdp", axis=0), sizes)
+
+
+def scatter_grads(grads, vector_grads):
+    devices = lax.axis_size("fsdp")
+    sizes = [v.shape[0] // devices for v in vector_grads]
+    joined = jnp.concatenate([v.reshape(devices, -1) for v in vector_grads], 1)
+    blocks = [jax.ShapeDtypeStruct((g.shape[0] // devices, g.shape[1]), g.dtype) for g in grads]
+    parts = [jax.ShapeDtypeStruct((size,), joined.dtype) for size in sizes]
+    if on_links(blocks, parts):
+        tiles = jnp.pad(joined, ((0, 0), (0, 1024 - joined.shape[1]))).reshape(2, 2, 4, 2, 8, 128)
+        *sums, vec = scatter_all([g.reshape(2, 2, -1, g.shape[1]) for g in grads], tiles)
+        vec = vec.reshape(1, 1024)
+    else:
+        sums = [
+            lax.psum_scatter(g.astype(jnp.float32), "fsdp", scatter_dimension=0, tiled=True) for g in grads
+        ]
+        vec = lax.psum_scatter(joined, "fsdp", scatter_dimension=0, tiled=True)
+    return sums, split_vectors(vec, sizes)
 
 
 def on_device(
@@ -329,72 +737,44 @@
     vis_slots = visible_index.reshape(seq_count, VIS)
     enc_seg = jnp.take_along_axis(seg_ids, vis_slots, 1)
     seq_index = jnp.arange(seq_count, dtype=jnp.int32)[:, None]
-    enc_full = (
-        lax.all_gather(enc_norm1_gain, "fsdp", axis=0, tiled=True),
-        lax.all_gather(enc_norm1_bias, "fsdp", axis=0, tiled=True),
-        lax.all_gather(enc_qkv, "fsdp", axis=0, tiled=True),
-        lax.all_gather(enc_query_bias, "fsdp", axis=0, tiled=True),
-        lax.all_gather(enc_value_bias, "fsdp", axis=0, tiled=True),
-        lax.all_gather(enc_out, "fsdp", axis=0, tiled=True),
-        lax.all_gather(enc_out_bias, "fsdp", axis=0, tiled=True),
-        lax.all_gather(enc_norm2_gain, "fsdp", axis=0, tiled=True),
-        lax.all_gather(enc_norm2_bias, "fsdp", axis=0, tiled=True),
-        lax.all_gather(enc_up, "fsdp", axis=0, tiled=True),
-        lax.all_gather(enc_up_bias, "fsdp", axis=0, tiled=True),
-        lax.all_gather(enc_down, "fsdp", axis=0, tiled=True),
-        lax.all_gather(enc_down_bias, "fsdp", axis=0, tiled=True),
-    )
+    matrices = (enc_qkv, enc_out, enc_up, enc_down, embed_weight, dec_qkv, dec_out, dec_up, dec_down)
+    vectors = (
+        enc_norm1_gain,
+        enc_norm1_bias,
+        enc_query_bias,
+        enc_value_bias,
+        enc_out_bias,
+        enc_norm2_gain,
+        enc_norm2_bias,
+        enc_up_bias,
+        enc_down_bias,
+        embed_bias,
+        mask_token,
+        dec_norm1_gain,
+        dec_norm1_bias,
+        dec_query_bias,
+        dec_value_bias,
+        dec_out_bias,
+        dec_norm2_gain,
+        dec_norm2_bias,
+        dec_up_bias,
+        dec_down_bias,
+    )
+    whole, whole_vec = gather_params(matrices, vectors)
+    (ng1, nb1, qb, vb, ob, ng2, nb2, ub, db, eb, mask, dng1, dnb1, dqb, dvb, dob, dng2, dnb2, dub, ddb) = whole_vec
+    enc_full = (ng1, nb1, whole[0], qb, vb, whole[1], ob, ng2, nb2, whole[2], ub, whole[3], db)
+    dec_full = (dng1, dnb1, whole[5], dqb, dvb, whole[6], dob, dng2, dnb2, whole[7], dub, whole[8], ddb)
     hidden, enc_saved = block_forward(widen(patches), enc_full, enc_seg, HEADS)
-    dec_full = (
-        lax.all_gather(embed_weight, "fsdp", axis=0, tiled=True),
-        lax.all_gather(embed_bias, "fsdp", axis=0, tiled=True),
-        lax.all_gather(mask_token, "fsdp", axis=0, tiled=True),
-        lax.all_gather(dec_norm1_gain, "fsdp", axis=0, tiled=True),
-        lax.all_gather(dec_norm1_bias, "fsdp", axis=0, tiled=True),
-        lax.all_gather(dec_qkv, "fsdp", axis=0, tiled=True),
-        lax.all_gather(dec_query_bias, "fsdp", axis=0, tiled=True),
-        lax.all_gather(dec_value_bias, "fsdp", axis=0, tiled=True),
-        lax.all_gather(dec_out, "fsdp", axis=0, tiled=True),
-        lax.all_gather(dec_out_bias, "fsdp", axis=0, tiled=True),
-        lax.all_gather(dec_norm2_gain, "fsdp", axis=0, tiled=True),
-        lax.all_gather(dec_norm2_bias, "fsdp", axis=0, tiled=True),
-        lax.all_gather(dec_up, "fsdp", axis=0, tiled=True),
-        lax.all_gather(dec_up_bias, "fsdp", axis=0, tiled=True),
-        lax.all_gather(dec_down, "fsdp", axis=0, tiled=True),
-        lax.all_gather(dec_down_bias, "fsdp", axis=0, tiled=True),
-    )
     hidden_low = hidden.astype(jnp.bfloat16)
-    embedded = jnp.dot(hidden_low, dec_full[0], preferred_element_type=jnp.float32) + widen(
-        dec_full[1]
-    )
+    embedded = jnp.dot(hidden_low, whole[4], preferred_element_type=jnp.float32) + eb
     embedded = embedded.reshape(seq_count, VIS, DD)
     dec_in = (
-        jnp.broadcast_to(widen(dec_full[2]), (seq_count, ROW, DD))
-        .at[seq_index, vis_slots]
-        .set(embedded)
+        jnp.broadcast_to(mask, (seq_count, ROW, DD)).at[seq_index, vis_slots].set(embedded)
     )
     dec_in = dec_in.reshape(seq_count * ROW, DD)
-    decoded, dec_saved = block_forward(dec_in, dec_full[3:], seg_ids, DHEADS)
-    dec_back = (
-        lax.all_gather(embed_weight, "fsdp", axis=0, tiled=True),
-        lax.all_gather(embed_bias, "fsdp", axis=0, tiled=True),
-        lax.all_gather(mask_token, "fsdp", axis=0, tiled=True),
-        lax.all_gather(dec_norm1_gain, "fsdp", axis=0, tiled=True),
-        lax.all_gather(dec_norm1_bias, "fsdp", axis=0, tiled=True),
-        lax.all_gather(dec_qkv, "fsdp", axis=0, tiled=True),
-        lax.all_gather(dec_query_bias, "fsdp", axis=0, tiled=True),
-        lax.all_gather(dec_value_bias, "fsdp", axis=0, tiled=True),
-        lax.all_gather(dec_out, "fsdp", axis=0, tiled=True),
-        lax.all_gather(dec_out_bias, "fsdp", axis=0, tiled=True),
-        lax.all_gather(dec_norm2_gain, "fsdp", axis=0, tiled=True),
-        lax.all_gather(dec_norm2_bias, "fsdp", axis=0, tiled=True),
-        lax.all_gather(dec_up, "fsdp", axis=0, tiled=True),
-        lax.all_gather(dec_up_bias, "fsdp", axis=0, tiled=True),
-        lax.all_gather(dec_down, "fsdp", axis=0, tiled=True),
-        lax.all_gather(dec_down_bias, "fsdp", axis=0, tiled=True),
-    )
+    decoded, dec_saved = block_forward(dec_in, dec_full, seg_ids, DHEADS)
     grad_dec_in, dec_grads = block_backward(
-        widen(cotangent), dec_back[3:], seg_ids, DHEADS, dec_saved
+        widen(cotangent), dec_full, seg_ids, DHEADS, dec_saved
     )
     grad_dec_in = grad_dec_in.reshape(seq_count, ROW, DD)
     shown_slots = jnp.zeros((seq_count, ROW), jnp.float32).at[seq_index, vis_slots].set(1.0)
@@ -404,60 +784,24 @@
     grad_embedded_low = grad_embedded.astype(jnp.bfloat16)
     grad_embed_w = jnp.einsum(
         "rd,re->de", hidden_low, grad_embedded_low, preferred_element_type=jnp.float32
-    )
+    ).astype(jnp.bfloat16)
     grad_hidden = jnp.einsum(
-        "re,de->rd", grad_embedded_low, dec_back[0], preferred_element_type=jnp.float32
-    )
-    dec_sums = (
-        lax.psum_scatter(grad_embed_w, "fsdp", scatter_dimension=0, tiled=True),
-        lax.psum_scatter(grad_embed_b, "fsdp", scatter_dimension=0, tiled=True),
-        lax.psum_scatter(grad_mask, "fsdp", scatter_dimension=0, tiled=True),
-        lax.psum_scatter(dec_grads[0], "fsdp", scatter_dimension=0, tiled=True),
-        lax.psum_scatter(dec_grads[1], "fsdp", scatter_dimension=0, tiled=True),
-        lax.psum_scatter(dec_grads[2], "fsdp", scatter_dimension=0, tiled=True),
-        lax.psum_scatter(dec_grads[3], "fsdp", scatter_dimension=0, tiled=True),
-        lax.psum_scatter(dec_grads[4], "fsdp", scatter_dimension=0, tiled=True),
-        lax.psum_scatter(dec_grads[5], "fsdp", scatter_dimension=0, tiled=True),
-        lax.psum_scatter(dec_grads[6], "fsdp", scatter_dimension=0, tiled=True),
-        lax.psum_scatter(dec_grads[7], "fsdp", scatter_dimension=0, tiled=True),
-        lax.psum_scatter(dec_grads[8], "fsdp", scatter_dimension=0, tiled=True),
-        lax.psum_scatter(dec_grads[9], "fsdp", scatter_dimension=0, tiled=True),
-        lax.psum_scatter(dec_grads[10], "fsdp", scatter_dimension=0, tiled=True),
-        lax.psum_scatter(dec_grads[11], "fsdp", scatter_dimension=0, tiled=True),
-        lax.psum_scatter(dec_grads[12], "fsdp", scatter_dimension=0, tiled=True),
-    )
-    enc_back = (
-        lax.all_gather(enc_norm1_gain, "fsdp", axis=0, tiled=True),
-        lax.all_gather(enc_norm1_bias, "fsdp", axis=0, tiled=True),
-        lax.all_gather(enc_qkv, "fsdp", axis=0, tiled=True),
-        lax.all_gather(enc_query_bias, "fsdp", axis=0, tiled=True),
-        lax.all_gather(enc_value_bias, "fsdp", axis=0, tiled=True),
-        lax.all_gather(enc_out, "fsdp", axis=0, tiled=True),
-        lax.all_gather(enc_out_bias, "fsdp", axis=0, tiled=True),
-        lax.all_gather(enc_norm2_gain, "fsdp", axis=0, tiled=True),
-        lax.all_gather(enc_norm2_bias, "fsdp", axis=0, tiled=True),
-        lax.all_gather(enc_up, "fsdp", axis=0, tiled=True),
-        lax.all_gather(enc_up_bias, "fsdp", axis=0, tiled=True),
-        lax.all_gather(enc_down, "fsdp", axis=0, tiled=True),
-        lax.all_gather(enc_down_bias, "fsdp", axis=0, tiled=True),
-    )
-    grad_patches, enc_grads = block_backward(grad_hidden, enc_back, enc_seg, HEADS, enc_saved)
-    enc_sums = (
-        lax.psum_scatter(enc_grads[0], "fsdp", scatter_dimension=0, tiled=True),
-        lax.psum_scatter(enc_grads[1], "fsdp", scatter_dimension=0, tiled=True),
-        lax.psum_scatter(enc_grads[2], "fsdp", scatter_dimension=0, tiled=True),
-        lax.psum_scatter(enc_grads[3], "fsdp", scatter_dimension=0, tiled=True),
-        lax.psum_scatter(enc_grads[4], "fsdp", scatter_dimension=0, tiled=True),
-        lax.psum_scatter(enc_grads[5], "fsdp", scatter_dimension=0, tiled=True),
-        lax.psum_scatter(enc_grads[6], "fsdp", scatter_dimension=0, tiled=True),
-        lax.psum_scatter(enc_grads[7], "fsdp", scatter_dimension=0, tiled=True),
-        lax.psum_scatter(enc_grads[8], "fsdp", scatter_dimension=0, tiled=True),
-        lax.psum_scatter(enc_grads[9], "fsdp", scatter_dimension=0, tiled=True),
-        lax.psum_scatter(enc_grads[10], "fsdp", scatter_dimension=0, tiled=True),
-        lax.psum_scatter(enc_grads[11], "fsdp", scatter_dimension=0, tiled=True),
-        lax.psum_scatter(enc_grads[12], "fsdp", scatter_dimension=0, tiled=True),
-    )
-    return (decoded.astype(jnp.bfloat16), grad_patches) + tuple(enc_sums) + tuple(dec_sums)
+        "re,de->rd", grad_embedded_low, whole[4], preferred_element_type=jnp.float32
+    )
+    grad_patches, enc_grads = block_backward(grad_hidden, enc_full, enc_seg, HEADS, enc_saved)
+    e, d = enc_grads, dec_grads
+    matrix_sums, vector_sums = scatter_grads(
+        (e[2], e[5], e[9], e[11], grad_embed_w, d[2], d[5], d[9], d[11]),
+        (e[0], e[1], e[3], e[4], e[6], e[7], e[8], e[10], e[12], grad_embed_b, grad_mask)
+        + (d[0], d[1], d[3], d[4], d[6], d[7], d[8], d[10], d[12]),
+    )
+    m, v = matrix_sums, vector_sums
+    return (
+        (decoded.astype(jnp.bfloat16), grad_patches)
+        + (v[0], v[1], m[0], v[2], v[3], m[1], v[4], v[5], v[6], m[2], v[7], m[3], v[8])
+        + (m[4], v[9], v[10])
+        + (v[11], v[12], m[5], v[13], v[14], m[6], v[15], v[16], v[17], m[7], v[18], m[8], v[19])
+    )
 
 
 def solution(mesh):

time: 1930 us -> 621 us (0.32)
  waiting for transfers between devices: 1400 us -> 0 us
  Pallas kernels: 0 us -> 265 us
  blocking collectives: 125 us -> 0 us
  matrix products: 279 us -> 241 us
    reduce_scatter x9 -> x0, waiting for transfers between devices: 1110 us -> none  [the longest x1 143 us: on_device(): lax.psum_scatter(dec_grads[9], 'fsdp', scatter_dimension=0, tiled=True)]
    pallas_call x0 -> x2, Pallas kernels: none -> 265 us  [the longest x1 133 us: gather_all(): pl.pallas_call(body, out_shape=out_shape, in_specs=[vmem] * (count + 1),...]
    all_gather x7 -> x0, waiting for transfers between devices: 194 us -> none  [the longest x1 53 us: on_device(): lax.all_gather(dec_down, 'fsdp', axis=0, tiled=True)]
    unnamed x18 -> x0, waiting for transfers between devices: 91.4 us -> none
    all_gather x2 -> x0, blocking collectives: 81.5 us -> none  [the longest x1 42.2 us: on_device(): lax.all_gather(dec_out, 'fsdp', axis=0, tiled=True)]
    unnamed x1 -> x0, blocking collectives: 43.4 us -> none
    reshape x0 -> x25, local copies, waits for them, and re-layouts: none -> 20.1 us  [the longest x20 14.6 us: scatter_grads(): joined = jnp.concatenate([v.reshape(devices, -1) for v in vector_grads], 1)]
    unnamed x266 -> x176, local copies, waits for them, and re-layouts: 38.9 us -> 22 us
  transfers between devices with their start and end apart: 17 -> 0, of which waited for: 15 -> 0; matrix products, arithmetic and copies ran while one was open for 9% -> 0% of each run, Pallas kernels for 0% -> 0%
where the time goes in v1:
time: 621 us; the launch traced here: 616 us
  Pallas kernels  265 us (43%)
  matrix products  241 us (39%)
  local copies, waits for them, and re-layouts  83.8 us (13%)
  other arithmetic  23.9 us (4%)
    pallas_call x1, Pallas kernels, gather_all(): pl.pallas_call(body, out_shape=out_shape, in_specs=[vmem] * (count + 1),...  133 us
    pallas_call x1, Pallas kernels, scatter_all(): pl.pallas_call(body, out_shape=out_shape, in_specs=[any_space] * (count +...  132 us
    dot_general x2, matrix products, attend_backward(): jnp.einsum('bhqk,bkhd->bqhd', grad_scores, key_heads, preferred_element_t...  43.7 us
    dot_general x2, matrix products, attend_backward(): jnp.einsum('bhqk,bqhd->bkhd', grad_scores, query_heads, preferred_element...  43.6 us
    dot_general x2, matrix products, block_forward(): jnp.dot(normed_two, w_up, preferred_element_type=jnp.float32)  25.3 us
    unnamed x176, local copies, waits for them, and re-layouts  22 us
    dot_general x2, matrix products, attend_backward(): jnp.einsum('bhqk,bqhd->bkhd', att_probs.astype(jnp.bfloat16), grad_heads,...  18.9 us
    dot_general x2, matrix products, attend_backward(): jnp.einsum('bqhd,bkhd->bhqk', grad_heads, value_heads, preferred_element_...  16.3 us

profile of v1, /device:TPU:0, one launch (start us, length us, event | category | flops | bytes accessed | tf_op | source)
XLA Modules:
  0.0 615.6 jit_solution(14755431485239752426)
XLA Ops:
  0.7 13.5 %concatenate.19 = bf16[512]{0:T(512)(128)(2,1)S(1)} concatenate(bf16[24]{0:T(256)(128)(2,1)} %param.37, bf16[24]{0:T(256)(128)(2,1)} %param.38, bf16[24]{0:T(256)(128)(2,1)} %param.40, bf16[24]{0:T(256)(128)(2,1)} %param.41, bf16[24]{0:T(256)(128)(2,1)} %param.43, bf16[24]{0:T(256)(128)(2,1)} %param.44, bf16[24]{0:T(256)(128)(2,1)} %param.45, bf16[96]{0:T(256)(128)(2,1)} %param.47, ...), dimensions={0} | concatenate | bytes 2048 | tf_op jit(solution)/shard_map/concatenate | solution.py:672
  15.5 3.4 gather_fusion
  22.2 3.7 scatter_custom_fusion.1
  27.7 132.5 %gather_params.1 = (bf16[2,2,192,2304]{3,2,1,0:T(8,128)(2,1)}, bf16[2,2,192,768]{3,2,1,0:T(8,128)(2,1)}, bf16[2,2,192,3072]{3,2,1,0:T(8,128)(2,1)}, bf16[2,2,768...) custom-call(bf16[24,2304]{1,0:T(8,128)(2,1)} %refs_0_.1, ...), custom_call_target="tpu_custom_call" | custom-call | tf_op jit(solution)/shard_map/gather_params/pallas_call | solution.py:452
  163.9 3.7 fusion.164
  183.2 15.0 %multiply_convert_fusion.2 = (bf16[384,3072]{1,0:T(8,128)(2,1)S(1)}, f32[384,3072]{1,0:T(8,128)}, f32[384,3072]{1,0:T(8,128)}) fusion(f32[3072]{0:T(1024)S(1)} %add.274, bf16[768,3072]{1,0:T(8,128)(2,1)S(1)} %bitcast.257, f32[384,768]{1,0:T(8,128)S(1)} %get-tuple-element.155, f32[768]{0:T(1024)S(1)} %add.271, f32[768]{0:T(1024)S(1)} %mul.369, ...), kind=kOutput, calls=%fused_computation.37 | convolution fusion | flops 1891270656 | bytes 17716224 | tf_op jit(solution)/shard_map/dot_general | solution.py:143
  201.6 2.7 scatter_fusion
  212.1 5.1 fusion.4
  217.3 5.2 fusion.3
  224.8 10.6 %fusion.78 = bf16[16,32,529]{2,1,0:T(8,128)(2,1)S(1)} fusion(bf16[529,16,32]{0,2,1:T(8,128)(2,1)S(1)} %bitcast.220, f32[16,529,529]{1,2,0:T(8,128)} %copy-done, f32[16,529]{1,0:T(8,128)S(1)} %fusion.3, f32[16,529]{1,0:T(8,128)S(1)} %get-tuple-element.157, pred[529,529]{0,1:T(8,128)(4,1)S(1)} %broadcast_compare_fusion), kind=kOutput, calls=%fused_computation.113 | convolution fusion | flops 309215296 | bytes 19340768 | tf_op jit(solution)/shard_map/bhqk,bkhd->bqhd/dot_general | solution.py:63
  236.9 10.3 %multiply_convert_fusion.3 = (bf16[529,2048]{1,0:T(8,128)(2,1)S(1)}, f32[529,2048]{1,0:T(8,128)S(1)}, f32[529,2048]{1,0:T(8,128)S(1)}) fusion(f32[2048]{0:T(1024)S(1)} %add.302, bf16[512,2048]{1,0:T(8,128)(2,1)S(1)} %bitcast.267, f32[529,512]{1,0:T(8,128)S(1)} %get-tuple-element.160, f32[512]{0:T(512)S(1)} %add.299, f32[512]{0:T(512)S(1)} %mul.385, ...), kind=kOutput, calls=%fused_computation.61 | convolution fusion | flops 1182251520 | bytes 14030984 | tf_op jit(solution)/shard_map/dot_general | solution.py:143
  247.2 3.2 fusion.190
  252.6 3.2 convolution_convert_fusion.4
  257.9 3.4 convolution_convert_fusion.5
  268.3 13.9 %fusion.176 = (f32[16,32]{1,0:T(8,128)S(1)}, bf16[1,529,16,32]{1,3,2,0:T(8,128)(2,1)}) fusion(bf16[529,16,32]{0,2,1:T(8,128)(2,1)} %bitcast.221, f32[16,529]{1,0:T(8,128)S(1)} %log_add_fusion, f32[16,529,529]{1,2,0:T(8,128)} %copy-done, pred[529,529]{0,1:T(8,128)(4,1)S(1)} %broadcast_compare_fusion), kind=kOutput, calls=%fused_computation.277 | convolution fusion | flops 305008192 | bytes 19308960 | tf_op jit(solution)/shard_map/bhqk,bqhd->bkhd/dot_general | solution.py:81
  282.8 12.3 %fusion.191 = f32[16,529,529]{1,2,0:T(8,128)} fusion(bf16[529,16,32]{0,2,1:T(8,128)(2,1)} %bitcast.222, bf16[529,16,32]{0,2,1:T(8,128)(2,1)} %bitcast.219), kind=kOutput, calls=%fused_computation.288 | convolution fusion | flops 286557184 | bytes 18993216 | tf_op jit(solution)/shard_map/bqhd,bkhd->bhqk/dot_general | solution.py:87
  295.1 30.5 %fusion.75 = bf16[16,32,529]{2,1,0:T(8,128)(2,1)} fusion(bf16[529,16,32]{0,2,1:T(8,128)(2,1)} %bitcast.218, f32[16,529,529]{1,2,0:T(8,128)} %fusion.191, f32[16,529]{1,0:T(8,128)S(1)} %log_add_fusion, f32[16,529,529]{1,2,0:T(8,128)} %copy-done, pred[529,529]{0,1:T(8,128)(4,1)S(1)} %broadcast_compare_fusion), kind=kOutput, calls=%fused_computation.112 | convolution fusion | flops 336089024 | bytes 37216736 | tf_op jit(solution)/shard_map/bhqk,bqhd->bkhd/dot_general | solution.py:95
  325.6 30.6 %fusion.177 = (f32[16,32]{1,0:T(8,128)S(1)}, bf16[1,529,16,32]{1,3,2,0:T(8,128)(2,1)}) fusion(bf16[529,16,32]{0,2,1:T(8,128)(2,1)} %bitcast.216, f32[16,529,529]{1,2,0:T(8,128)} %fusion.191, f32[16,529]{1,0:T(8,128)S(1)} %log_add_fusion, f32[16,529,529]{1,2,0:T(8,128)} %copy-done, pred[529,529]{0,1:T(8,128)(4,1)S(1)} %broadcast_compare_fusion), kind=kOutput, calls=%fused_computation.278 | convolution fusion | flops 336359360 | bytes 37218784 | tf_op jit(solution)/shard_map/bhqk,bkhd->bqhd/dot_general | solution.py:92
  356.3 3.7 multiply_reduce_fusion.6
  360.0 2.9 convolution_convert_fusion.3
  376.5 8.1 %fusion.189 = (f32[3072]{0:T(1024)S(1)}, bf16[384,3072]{1,0:T(8,128)(2,1)S(1)}) fusion(f32[384,3072]{1,0:T(8,128)} %get-tuple-element.99, f32[384,3072]{1,0:T(8,128)} %get-tuple-element.156, bf16[3072,768]{1,0:T(8,128)(2,1)} %bitcast.261, f32[384,768]{1,0:T(8,128)S(1)} %fusion.130), kind=kOutput, calls=%fused_computation.286 | convolution fusion | flops 1829925888 | bytes 17707008 | tf_op jit(solution)/shard_map/rw,fw->rf/dot_general | solution.py:196
  384.7 2.8 multiply_reduce_fusion.2
  398.9 2.9 convolution_convert_fusion.6
  401.8 5.1 fusion.178
  408.2 7.2 %convolution_convert_fusion.1 = bf16[768,3072]{1,0:T(8,128)(2,1)} fusion(bf16[384,3072]{1,0:T(8,128)(2,1)} %copy-done.75, f32[384,768]{1,0:T(8,128)} %copy-done.5, f32[768]{0:T(1024)} %copy-done.64, f32[768]{0:T(1024)} %copy-done.56, f32[384]{0:T(512)} %copy-done.58, f32[384]{0:T(512)} %copy-done.47), kind=kOutput, calls=%fused_computation.33 | convolution fusion | flops 1815773184 | bytes 8266752 | tf_op jit(solution)/shard_map/rd,rf->df/dot_general | solution.py:200
  415.5 4.6 convolution_convert_fusion
  420.0 4.0 fusion.192
  424.1 13.1 %fusion.84 = bf16[12,64,384]{2,1,0:T(8,128)(2,1)} fusion(bf16[384,12,64]{0,2,1:T(8,128)(2,1)S(1)} %bitcast.228, f32[12,384,384]{1,2,0:T(8,128)} %fusion.192, f32[12,384,384]{1,2,0:T(8,128)} %copy-done.1, f32[12,384]{1,0:T(8,128)} %log_add_fusion.1), kind=kOutput, calls=%fused_computation.120 | convolution fusion | flops 239178624 | bytes 15353856 | tf_op jit(solution)/shard_map/bhqk,bqhd->bkhd/dot_general | solution.py:95
  437.2 13.1 %fusion.179 = (f32[12,64]{1,0:T(8,128)S(1)}, bf16[1,384,12,64]{1,3,2,0:T(8,128)(2,1)}) fusion(bf16[384,12,64]{0,2,1:T(8,128)(2,1)S(1)} %bitcast.226, f32[12,384,384]{1,2,0:T(8,128)} %fusion.192, f32[12,384,384]{1,2,0:T(8,128)} %copy-done.1, f32[12,384]{1,0:T(8,128)} %log_add_fusion.1), kind=kOutput, calls=%fused_computation.280 | convolution fusion | flops 239472768 | bytes 15356928 | tf_op jit(solution)/shard_map/bhqk,bkhd->bqhd/dot_general | solution.py:92
  450.4 4.1 fusion.168
  458.1 5.6 convolution_convert_fusion.2
  463.7 132.0 %scatter_grads.1 = (f32[24,2304]{1,0:T(8,128)}, f32[24,768]{1,0:T(8,128)}, f32[24,3072]{1,0:T(8,128)}, f32[96,768]{1,0:T(8,128)}, f32[24,512]{1,0:T(8,128)}, /*i...) custom-call(bf16[2,2,192,2304]{3,2,1,0:T(8,128)(2,1)} %bitcast.213, ...), custom_call_target="tpu_custom_call" | custom-call | tf_op jit(solution)/shard_map/scatter_grads/pallas_call | solution.py:640
  (301 shorter events, 101.0 us)
Async XLA Ops:
  0.7 163.2 %copy-start.3 = (bf16[384,768]{1,0:T(8,128)(2,1)S(1)}, bf16[384,768]{1,0:T(8,128)(2,1)}, u32[]{:S(2)}) copy-start(bf16[384,768]{1,0:T(8,128)(2,1)} %param.33) | copy-start | bytes 1769476
  20.8 146.8 %copy-start.43 = (f32[384]{0:T(512)}, f32[384]{0:T(512)S(1)}, u32[]{:S(2)}) copy-start(f32[384]{0:T(512)S(1)} %broadcast_multiply_fusion.3) | copy-start | bytes 4612
  22.2 138.0 %copy-start.49 = (f32[384]{0:T(512)}, f32[384]{0:T(512)S(1)}, u32[]{:S(2)}) copy-start(f32[384]{0:T(512)S(1)} %fusion.92) | copy-start | bytes 4612
  22.2 145.4 %copy-start.45 = (f32[384]{0:T(512)}, f32[384]{0:T(512)S(1)}, u32[]{:S(2)}) copy-start(f32[384]{0:T(512)S(1)} %fusion.138) | copy-start | bytes 4612
  161.8 21.3 %copy-start.56 = (f32[768]{0:T(1024)}, f32[768]{0:T(1024)S(1)}, u32[]{:S(2)}) copy-start(f32[768]{0:T(1024)S(1)} %mul.369) | copy-start | bytes 9220
  161.9 21.2 %copy-start.64 = (f32[768]{0:T(1024)}, f32[768]{0:T(1024)S(1)}, u32[]{:S(2)}) copy-start(f32[768]{0:T(1024)S(1)} %add.271) | copy-start | bytes 9220
  163.2 41.6 %copy-start.60 = (f32[512]{0:T(512)}, f32[512]{0:T(512)S(1)}, u32[]{:S(2)}) copy-start(f32[512]{0:T(512)S(1)} %mul.378) | copy-start | bytes 6148
  163.3 41.5 %copy-start.65 = (f32[512]{0:T(512)}, f32[512]{0:T(512)S(1)}, u32[]{:S(2)}) copy-start(f32[512]{0:T(512)S(1)} %add.285) | copy-start | bytes 6148
  180.3 17.9 %copy-start.17 = (bf16[12,64,384]{2,1,0:T(8,128)(2,1)}, bf16[12,64,384]{2,1,0:T(8,128)(2,1)S(1)}, u32[]{:S(2)}) copy-start(bf16[12,64,384]{2,1,0:T(8,128)(2,1)S(1)} %fusion.83) | copy-start | bytes 1769476
  182.0 16.2 %slice-start.4 = ((s8[4718592]{0:T(1024)(128)(4,1)}), s8[524288]{0:T(1024)(128)(4,1)S(1)}, s32[]{:S(2)}) async-start(s8[4718592]{0:T(1024)(128)(4,1)} %bitcast.262), calls=%async_computation.4 | async-start | bytes 1048576
  182.8 15.4 %copy-start.5 = (f32[384,768]{1,0:T(8,128)}, f32[384,768]{1,0:T(8,128)S(1)}, u32[]{:S(2)}) copy-start(f32[384,768]{1,0:T(8,128)S(1)} %get-tuple-element.155) | copy-start | bytes 3538948
  182.8 15.4 %copy-start.47 = (f32[384]{0:T(512)}, f32[384]{0:T(512)S(1)}, u32[]{:S(2)}) copy-start(f32[384]{0:T(512)S(1)} %broadcast_multiply_fusion.2) | copy-start | bytes 4612
  183.1 15.1 %copy-start.51 = (f32[384]{0:T(512)}, f32[384]{0:T(512)S(1)}, u32[]{:S(2)}) copy-start(f32[384]{0:T(512)S(1)} %multiply_reduce_fusion.4) | copy-start | bytes 4612
  183.1 15.1 %copy-start.58 = (f32[384]{0:T(512)}, f32[384]{0:T(512)S(1)}, u32[]{:S(2)}) copy-start(f32[384]{0:T(512)S(1)} %fusion.139) | copy-start | bytes 4612
  183.2 15.1 %slice-start.5 = ((s8[4718592]{0:T(1024)(128)(4,1)}), s8[4194304]{0:T(1024)(128)(4,1)S(1)}, s32[]{:S(2)}) async-start(s8[4718592]{0:T(1024)(128)(4,1)} %bitcast.262), calls=%async_computation.5 | async-start | bytes 8388608
  224.7 10.6 %copy-start.14 = (bf16[2,2,128,512]{3,2,1,0:T(8,128)(2,1)S(1)}, bf16[2,2,128,512]{3,2,1,0:T(8,128)(2,1)}, u32[]{:S(2)}) copy-start(bf16[2,2,128,512]{3,2,1,0:T(8,128)(2,1)} %get-tuple-element.58) | copy-start | bytes 1572868
  236.9 10.3 %copy-start.20 = (bf16[529,512]{1,0:T(8,128)(2,1)S(1)}, bf16[529,512]{1,0:T(8,128)(2,1)}, u32[]{:S(2)}) copy-start(bf16[529,512]{1,0:T(8,128)(2,1)} %param.36) | copy-start | bytes 1625092
  236.9 10.3 %copy-start.69 = (bf16[2,2,512,512]{3,2,1,0:T(8,128)(2,1)S(1)}, bf16[2,2,512,512]{3,2,1,0:T(8,128)(2,1)}, u32[]{:S(2)}) copy-start(bf16[2,2,512,512]{3,2,1,0:T(8,128)(2,1)} %get-tuple-element.60) | copy-start | bytes 6291460
  325.6 30.6 %copy-start.40 = (f32[529]{0:T(1024)S(1)}, f32[529]{0:T(1024)}, u32[]{:S(2)}) copy-start(f32[529]{0:T(1024)} %copy-done.39) | copy-start | bytes 6352
  325.6 30.6 %copy-start.54 = (f32[529]{0:T(1024)S(1)}, f32[529]{0:T(1024)}, u32[]{:S(2)}) copy-start(f32[529]{0:T(1024)} %copy-done.53) | copy-start | bytes 6352
  325.6 30.6 %copy-start.61 = (f32[512]{0:T(512)S(1)}, f32[512]{0:T(512)}, u32[]{:S(2)}) copy-start(f32[512]{0:T(512)} %copy-done.60) | copy-start | bytes 6148
  362.9 7.6 %copy-start.2 = (s32[384]{0:T(512)S(1)}, s32[384]{0:T(512)}, u32[]{:S(2)}) copy-start(s32[384]{0:T(512)} %get-tuple-element.86) | copy-start | bytes 4612
  373.2 11.3 %slice-start.2 = ((s8[4718592]{0:T(1024)(128)(4,1)}), s8[4194304]{0:T(1024)(128)(4,1)S(1)}, s32[]{:S(2)}) async-start(s8[4718592]{0:T(1024)(128)(4,1)} %bitcast.258), calls=%async_computation.2 | async-start | bytes 8388608
  376.4 8.1 %copy-start.6 = (f32[384,768]{1,0:T(8,128)S(1)}, f32[384,768]{1,0:T(8,128)}, u32[]{:S(2)}) copy-start(f32[384,768]{1,0:T(8,128)} %copy-done.5) | copy-start | bytes 3538948
  376.5 8.1 %copy-start.48 = (f32[384]{0:T(512)S(1)}, f32[384]{0:T(512)}, u32[]{:S(2)}) copy-start(f32[384]{0:T(512)} %copy-done.47) | copy-start | bytes 4612
  376.5 8.1 %copy-start.57 = (f32[768]{0:T(1024)S(1)}, f32[768]{0:T(1024)}, u32[]{:S(2)}) copy-start(f32[768]{0:T(1024)} %copy-done.56) | copy-start | bytes 9220
  376.5 8.1 %copy-start.59 = (f32[384]{0:T(512)S(1)}, f32[384]{0:T(512)}, u32[]{:S(2)}) copy-start(f32[384]{0:T(512)} %copy-done.58) | copy-start | bytes 4612
  376.5 8.1 %slice-start.3 = ((s8[4718592]{0:T(1024)(128)(4,1)}), s8[524288]{0:T(1024)(128)(4,1)S(1)}, s32[]{:S(2)}) async-start(s8[4718592]{0:T(1024)(128)(4,1)} %bitcast.258), calls=%async_computation.3 | async-start | bytes 1048576
  424.1 13.1 %copy-start.10 = (bf16[384,768]{0,1:T(8,128)(2,1)S(1)}, bf16[384,768]{0,1:T(8,128)(2,1)}, u32[]{:S(2)}) copy-start(bf16[384,768]{0,1:T(8,128)(2,1)} %copy-done.9) | copy-start | bytes 1769476
  437.2 13.2 %copy-start.4 = (bf16[384,768]{1,0:T(8,128)(2,1)S(1)}, bf16[384,768]{1,0:T(8,128)(2,1)}, u32[]{:S(2)}) copy-start(bf16[384,768]{1,0:T(8,128)(2,1)} %param.33) | copy-start | bytes 1769476
  437.2 13.2 %copy-start.38 = (f32[768]{0:T(1024)S(1)}, f32[768]{0:T(1024)}, u32[]{:S(2)}) copy-start(f32[768]{0:T(1024)} %copy-done.37) | copy-start | bytes 9220
  437.2 13.2 %copy-start.44 = (f32[384]{0:T(512)S(1)}, f32[384]{0:T(512)}, u32[]{:S(2)}) copy-start(f32[384]{0:T(512)} %copy-done.43) | copy-start | bytes 4612
  (50 other events, 174.1 us)
